TPU v7x, 32 devices: a whole 2x2x4 slice. The times are simulated.
32 devices in a mesh: dp: 8 (over y, x, core), tensor: 4 (over z).
Axes of the slice: x: 2, y: 2, z: 4, core: 2. Of those that a mesh axis runs over, the one named last changes fastest.
Arguments:
- inputs: bfloat16 [12288, 1536], P(('dp', 'tensor')), may hold values from -6 to 6
- cotangent: bfloat16 [12288, 1536], P(('dp', 'tensor')), may hold values from -6 to 6
- seq_lengths: int32 [8, 3], P('dp'), may hold values from 1 to 1154, 1536 in all within a row
- norm_gain: float32 [1536], replicated, may hold values from 0.5 to 1.5
- w_z: bfloat16 [1536, 3072], P('dp', 'tensor'), may hold values from -0.15625 to 0.15625
- w_x: bfloat16 [1536, 3072], P('dp', 'tensor'), may hold values from -0.15625 to 0.15625
- w_bc: bfloat16 [1536, 256], P('dp'), may hold values from -0.15625 to 0.15625
- w_dt: bfloat16 [1536, 48], P('dp', 'tensor'), may hold values from -0.15625 to 0.15625
- conv_x: float32 [4, 3072], P(None, 'tensor'), may hold values from -3 to 3
- conv_x_bias: float32 [3072], P('tensor'), may hold values from -3 to 3
- conv_bc: float32 [4, 256], replicated, may hold values from -3 to 3
- conv_bc_bias: float32 [256], replicated, may hold values from -3 to 3
- dt_bias: float32 [48], P('tensor'), may hold values from -7 to -1
- a_log: float32 [48], P('tensor'), may hold values from -1 to 2
- d_skip: float32 [48], P('tensor'), may hold values from 0.5 to 1.5
- gate_gain: float32 [3072], P('tensor'), may hold values from 0.5 to 1.5
- w_out: bfloat16 [3072, 1536], P('tensor', 'dp'), may hold values from -0.109375 to 0.109375
Outputs:
- outputs: bfloat16 [12288, 1536], P(('dp', 'tensor'))
- grad_inputs: bfloat16 [12288, 1536], P(('dp', 'tensor'))
- grad_norm_gain: float32 [1536], replicated
- grad_w_z: float32 [1536, 3072], P('dp', 'tensor')
- grad_w_x: float32 [1536, 3072], P('dp', 'tensor')
- grad_w_bc: float32 [1536, 256], P('dp')
- grad_w_dt: float32 [1536, 48], P('dp', 'tensor')
- grad_conv_x: float32 [4, 3072], P(None, 'tensor')
- grad_conv_x_bias: float32 [3072], P('tensor')
- grad_conv_bc: float32 [4, 256], replicated
- grad_conv_bc_bias: float32 [256], replicated
- grad_dt_bias: float32 [48], P('tensor')
- grad_a_log: float32 [48], P('tensor')
- grad_d_skip: float32 [48], P('tensor')
- grad_gate_gain: float32 [3072], P('tensor')
- grad_w_out: float32 [3072, 1536], P('tensor', 'dp')
Inputs may be any that keep to these rules, and one draw needn't show every extreme that they name: `seq_lengths`: each row lists the lengths of the sequences of one group in token order; they sum to 1536, and the largest is exactly 1154.
All inputs are finite; a program needn't handle non-finite values.
Results may differ from a plain program's by a relative error of at most 0.019.
Values may be sent and summed in bfloat16 or wider, within the bound.
A program may use at most 384 MiB of HBM per device.

v0:
```python
from functools import partial

import jax
import jax.numpy as jnp
from jax import lax
from jax.sharding import PartitionSpec as P

SPAN = 256


epsilon = 1e-05
highest = lax.Precision.HIGHEST


def silu(values):
    return values * jax.nn.sigmoid(values)


def silu_slope(values):
    sigma = jax.nn.sigmoid(values)
    return sigma * (1.0 + values * (1.0 - sigma))


def dot_rows(left, right):
    return lax.dot_general(
        left, right, (((0,), (0,)), ((), ())), preferred_element_type=jnp.float32
    )


def dot_cols(left, right):
    return lax.dot_general(
        left, right, (((1,), (1,)), ((), ())), preferred_element_type=jnp.float32
    )


def segments_of(lengths_row, count):
    ends = jnp.cumsum(lengths_row)
    places = jnp.arange(count, dtype=jnp.int32)
    return jnp.sum((ends[None, :] <= places[:, None]).astype(jnp.int32), axis=1)


def behind(values, offset, fill_value):
    padding = jnp.full((offset,) + values.shape[1:], fill_value, values.dtype)
    return jnp.concatenate([padding, values[:-offset]], axis=0)


def ahead(values, offset):
    padding = jnp.zeros((offset,) + values.shape[1:], values.dtype)
    return jnp.concatenate([values[offset:], padding], axis=0)


def lag_masks(segment, taps):
    masks = [jnp.ones(segment.shape, jnp.float32)]
    for offset in range(1, taps):
        masks.append((behind(segment, offset, -1) == segment).astype(jnp.float32))
    return masks


def conv_forward(values, kernel, bias_row, masks):
    running = bias_row[None, :] + kernel[0][None, :] * values
    for offset in range(1, kernel.shape[0]):
        running = (
            running + kernel[offset][None, :] * behind(values, offset, 0.0) * masks[offset][:, None]
        )
    return running


def conv_backward(upstream, values, kernel, masks, row_select):
    grad_values = kernel[0][None, :] * upstream
    picked = upstream * row_select[:, None]
    grad_taps = [jnp.sum(picked * values, axis=0)]
    for offset in range(1, kernel.shape[0]):
        masked = upstream * masks[offset][:, None]
        grad_values = grad_values + kernel[offset][None, :] * ahead(masked, offset)
        grad_taps.append(
            jnp.sum(picked * masks[offset][:, None] * behind(values, offset, 0.0), axis=0)
        )
    return (grad_values, jnp.stack(grad_taps), jnp.sum(picked, axis=0))


def block_step(rate, carry, block):
    state_now, prev_segment = carry
    x_block, b_block, c_block, step_block, seg_block = block
    length = x_block.shape[0]
    log_decay = jnp.cumsum(step_block * rate[None, :], axis=0)
    places = jnp.arange(length, dtype=jnp.int32)
    visible = (places[:, None] >= places[None, :]) & (seg_block[:, None] == seg_block[None, :])
    gaps = log_decay[:, None, :] - log_decay[None, :, :]
    decays = jnp.where(visible[:, :, None], jnp.exp(jnp.where(visible[:, :, None], gaps, 0.0)), 0.0)
    intersection = jnp.dot(c_block, b_block.T, precision=highest)
    mixing = intersection[:, :, None] * decays * step_block[None, :, :]
    local_part = jnp.einsum("tsh,shp->thp", mixing, x_block, precision=highest)
    carry_mask = (seg_block == prev_segment).astype(jnp.float32)
    state_read = jnp.einsum("tn,hpn->thp", c_block, state_now, precision=highest)
    state_part = state_read * (carry_mask[:, None] * jnp.exp(log_decay))[:, :, None]
    last_seg = seg_block[length - 1]
    tail_weight = (
        (seg_block == last_seg).astype(jnp.float32)[:, None]
        * jnp.exp(log_decay[length - 1][None, :] - log_decay)
        * step_block
    )
    fresh_state = jnp.einsum("sh,shp,sn->hpn", tail_weight, x_block, b_block, precision=highest)
    kept_state = (prev_segment == last_seg).astype(jnp.float32) * jnp.exp(log_decay[length - 1])
    new_state = fresh_state + kept_state[:, None, None] * state_now
    return ((new_state, last_seg), local_part + state_part)


def run_scan(heads_x, b_map, c_map, steps_dt, log_rates, segment):
    count, heads, width = heads_x.shape
    rate = -jnp.exp(log_rates)
    blocks = count // SPAN
    pieces = (
        heads_x.reshape(blocks, SPAN, heads, width),
        b_map.reshape(blocks, SPAN, -1),
        c_map.reshape(blocks, SPAN, -1),
        steps_dt.reshape(blocks, SPAN, heads),
        segment.reshape(blocks, SPAN),
    )
    begin = (jnp.zeros((heads, width, b_map.shape[1]), jnp.float32), jnp.int32(-1))
    _, ys = lax.scan(partial(block_step, rate), begin, pieces)
    return ys.reshape(count, heads, width)


def widen(local_part, parts, position, axis_index):
    piece_len = local_part.shape[axis_index]
    extent = list(local_part.shape)
    extent[axis_index] = piece_len * parts
    blank = jnp.zeros(tuple(extent), jnp.float32)
    return lax.dynamic_update_slice_in_dim(blank, local_part, position * piece_len, axis_index)


def narrow(whole, parts, position, axis_index):
    piece_len = whole.shape[axis_index] // parts
    return lax.dynamic_slice_in_dim(whole, position * piece_len, piece_len, axis_index)


def local(
    inputs,
    cotangent,
    seq_lengths,
    norm_gain,
    w_z,
    w_x,
    w_bc,
    w_dt,
    conv_x,
    conv_x_bias,
    conv_bc,
    conv_bc_bias,
    dt_bias,
    a_log,
    d_skip,
    gate_gain,
    w_out,
):
    local_rows, width = inputs.shape
    parts = lax.axis_size("tensor")
    position = lax.axis_index("tensor")
    group = local_rows * parts
    heads_here = dt_bias.shape[0]
    inner_here = w_z.shape[1]
    head_width = inner_here // heads_here
    state_size = w_bc.shape[1] // 2
    inner_all = inner_here * parts
    segment = segments_of(seq_lengths[0], group)
    masks = lag_masks(segment, conv_x.shape[0])
    places = jnp.arange(group, dtype=jnp.int32)
    own_rows = ((places >= position * local_rows) & (places < (position + 1) * local_rows)).astype(
        jnp.float32
    )
    all_rows = jnp.ones((group,), jnp.float32)
    input_f = inputs.astype(jnp.float32)
    in_scale = lax.rsqrt(jnp.mean(input_f * input_f, axis=1, keepdims=True) + epsilon)
    normed = (input_f * in_scale * norm_gain[None, :]).astype(jnp.bfloat16)
    tokens, pulled = (
        lax.all_gather(normed, "tensor", axis=0, tiled=True),
        lax.all_gather(cotangent, "tensor", axis=0, tiled=True),
    )
    shards = (
        lax.all_gather(w_z, "dp", axis=0, tiled=True),
        lax.all_gather(w_x, "dp", axis=0, tiled=True),
        lax.all_gather(w_bc, "dp", axis=0, tiled=True),
        lax.all_gather(w_dt, "dp", axis=0, tiled=True),
    )
    columns = tokens
    zgate, xpre, bcpre, dtraw = tuple(
        (jnp.dot(columns, shard_rows, preferred_element_type=jnp.float32) for shard_rows in shards)
    )
    conv_xv = conv_forward(xpre, conv_x, conv_x_bias, masks)
    scanned = silu(conv_xv).astype(jnp.bfloat16)
    conv_bcv = conv_forward(bcpre, conv_bc, conv_bc_bias, masks)
    maps = silu(conv_bcv).astype(jnp.bfloat16)
    heads_x = scanned.astype(jnp.float32).reshape(group, heads_here, head_width)
    b_map = maps[:, :state_size].astype(jnp.float32)
    c_map = maps[:, state_size:].astype(jnp.float32)
    dt_input = dtraw + dt_bias[None, :]
    steps_dt = jax.nn.softplus(dt_input)
    scan_out, scan_pull = jax.vjp(
        lambda hx, bmat, cmat, sdt, lrate: run_scan(hx, bmat, cmat, sdt, lrate, segment),
        heads_x,
        b_map,
        c_map,
        steps_dt,
        a_log,
    )
    result = scan_out + d_skip[None, :, None] * heads_x
    flat_result = result.reshape(group, inner_here)
    gate_act = silu(zgate)
    gated = flat_result * gate_act
    squares = lax.psum(jnp.sum(gated * gated, axis=1), "tensor")
    gscale = lax.rsqrt(squares / inner_all + epsilon)[:, None]
    mixed = (gated * gscale * gate_gain[None, :]).astype(jnp.bfloat16)
    branch_part = jnp.dot(
        mixed, lax.all_gather(w_out, "dp", axis=1, tiled=True), preferred_element_type=jnp.float32
    )
    branch = lax.psum_scatter(
        branch_part.astype(jnp.bfloat16), "tensor", scatter_dimension=0, tiled=True
    ).astype(jnp.float32)
    outputs = (input_f + branch).astype(jnp.bfloat16)
    grad_w_out = dot_rows(mixed, pulled)
    columns = pulled
    dmixed = dot_cols(columns, lax.all_gather(w_out, "dp", axis=1, tiled=True))
    grad_gate_gain = jnp.sum(dmixed * gated * gscale, axis=0)
    dgain_side = dmixed * gate_gain[None, :]
    cross = lax.psum(jnp.sum(dgain_side * gated, axis=1), "tensor")[:, None]
    dgated = gscale * dgain_side - gated * gscale * gscale * gscale * cross / inner_all
    dresult = (dgated * gate_act).reshape(group, heads_here, head_width)
    dzgate = dgated * flat_result * silu_slope(zgate)
    grad_d_skip = jnp.sum(dresult * heads_x, axis=(0, 2))
    dheads, dbmap, dcmap, dsteps, grad_a_log = scan_pull(dresult)
    dheads = dheads + dresult * d_skip[None, :, None]
    dmaps = lax.psum(jnp.concatenate([dbmap, dcmap], axis=1).astype(jnp.bfloat16), "tensor").astype(
        jnp.float32
    )
    dconv_x = dheads.reshape(group, inner_here) * silu_slope(conv_xv)
    dxpre, grad_conv_x, grad_conv_x_bias = conv_backward(dconv_x, xpre, conv_x, masks, all_rows)
    dconv_bc = dmaps * silu_slope(conv_bcv)
    dbcpre, grad_conv_bc, grad_conv_bc_bias = conv_backward(
        dconv_bc, bcpre, conv_bc, masks, own_rows
    )
    ddt_input = dsteps * jax.nn.sigmoid(dt_input)
    grad_dt_bias = jnp.sum(ddt_input, axis=0)
    dz_low = dzgate.astype(jnp.bfloat16)
    dx_low = dxpre.astype(jnp.bfloat16)
    dbc_low = dbcpre.astype(jnp.bfloat16)
    ddt_low = ddt_input.astype(jnp.bfloat16)
    dbc_own = dbc_low * own_rows[:, None].astype(jnp.bfloat16)
    grad_w_z = dot_rows(tokens, dz_low)
    grad_w_x = dot_rows(tokens, dx_low)
    grad_w_bc = dot_rows(tokens, dbc_low)
    grad_w_dt = dot_rows(tokens, ddt_low)
    shards = (
        lax.all_gather(w_z, "dp", axis=0, tiled=True),
        lax.all_gather(w_x, "dp", axis=0, tiled=True),
        lax.all_gather(w_bc, "dp", axis=0, tiled=True),
        lax.all_gather(w_dt, "dp", axis=0, tiled=True),
    )
    contribution = (
        dot_cols(dz_low, shards[0])
        + dot_cols(dx_low, shards[1])
        + dot_cols(dbc_own, shards[2])
        + dot_cols(ddt_low, shards[3])
    )
    dnormed_own = lax.psum_scatter(
        contribution.astype(jnp.bfloat16), "tensor", scatter_dimension=0, tiled=True
    ).astype(jnp.float32)
    grad_norm_gain = jnp.sum(dnormed_own * input_f * in_scale, axis=0)
    dnorm_side = dnormed_own * norm_gain[None, :]
    dinput = (
        in_scale * dnorm_side
        - input_f
        * in_scale
        * in_scale
        * in_scale
        * jnp.sum(dnorm_side * input_f, axis=1, keepdims=True)
        / width
        + cotangent.astype(jnp.float32)
    )
    grad_inputs = dinput.astype(jnp.bfloat16)
    sum_z, sum_x, sum_bc, sum_dt, sum_out = (
        lax.psum_scatter(
            grad_w_z.astype(jnp.bfloat16), "dp", scatter_dimension=0, tiled=True
        ).astype(jnp.float32),
        lax.psum_scatter(
            grad_w_x.astype(jnp.bfloat16), "dp", scatter_dimension=0, tiled=True
        ).astype(jnp.float32),
        lax.psum_scatter(
            grad_w_bc.astype(jnp.bfloat16), "dp", scatter_dimension=0, tiled=True
        ).astype(jnp.float32),
        lax.psum_scatter(
            grad_w_dt.astype(jnp.bfloat16), "dp", scatter_dimension=0, tiled=True
        ).astype(jnp.float32),
        lax.psum_scatter(
            grad_w_out.astype(jnp.bfloat16), "dp", scatter_dimension=1, tiled=True
        ).astype(jnp.float32),
    )
    totals = lax.psum(
        (
            grad_norm_gain,
            widen(grad_conv_x, parts, position, 1),
            widen(grad_conv_x_bias, parts, position, 0),
            grad_conv_bc,
            grad_conv_bc_bias,
            widen(grad_dt_bias, parts, position, 0),
            widen(grad_a_log, parts, position, 0),
            widen(grad_d_skip, parts, position, 0),
            widen(grad_gate_gain, parts, position, 0),
        ),
        ("dp", "tensor"),
    )
    return (
        outputs,
        grad_inputs,
        totals[0],
        sum_z,
        sum_x,
        sum_bc,
        sum_dt,
        narrow(totals[1], parts, position, 1),
        narrow(totals[2], parts, position, 0),
        totals[3],
        totals[4],
        narrow(totals[5], parts, position, 0),
        narrow(totals[6], parts, position, 0),
        narrow(totals[7], parts, position, 0),
        narrow(totals[8], parts, position, 0),
        sum_out,
    )


def solution(mesh):
    return jax.shard_map(
        local,
        mesh=mesh,
        in_specs=(
            P(("dp", "tensor"), None),
            P(("dp", "tensor"), None),
            P("dp", None),
            P(),
            P("dp", "tensor"),
            P("dp", "tensor"),
            P("dp", None),
            P("dp", "tensor"),
            P(None, "tensor"),
            P("tensor"),
            P(),
            P(),
            P("tensor"),
            P("tensor"),
            P("tensor"),
            P("tensor"),
            P("tensor", "dp"),
        ),
        out_specs=(
            P(("dp", "tensor"), None),
            P(("dp", "tensor"), None),
            P(),
            P("dp", "tensor"),
            P("dp", "tensor"),
            P("dp", None),
            P("dp", "tensor"),
            P(None, "tensor"),
            P("tensor"),
            P(),
            P(),
            P("tensor"),
            P("tensor"),
            P("tensor"),
            P("tensor"),
            P("tensor", "dp"),
        ),
        check_vma=False,
    )
```

profile of v0, /device:TPU:8, one launch (start us, length us, event | category | flops | bytes accessed | tf_op | source)
XLA Modules:
  0.0 1270.3 jit_solution(16615490658532378919)
XLA Ops:
  15.1 10.4 all_gather.29
  25.9 9.2 all-gather
  35.6 64.6 %all-gather.7.cloned.1.call-done = bf16[1536,1536]{1,0:T(8,128)(2,1)} async-done(((bf16[384,1536]{1,0:T(8,128)(2,1)}), bf16[1536,1536]{1,0:T(8,128)(2,1)}) %all-gather.7.cloned.1.call-update) | async-done | bytes 4718608 | tf_op jit(solution)/shard_map/all_gather | solution.py:176
  100.1 4.3 compare_select_fusion
  104.5 27.8 %all-gather.9.cloned.1.call-done = bf16[1536,768]{1,0:T(8,128)(2,1)} async-done(((bf16[192,768]{1,0:T(8,128)(2,1)}), bf16[1536,768]{1,0:T(8,128)(2,1)}) %all-gather.9.cloned.1.call-update) | async-done | bytes 2359312 | tf_op jit(solution)/shard_map/all_gather | solution.py:181
  132.3 6.4 fusion.177
  138.7 6.4 fusion.157
  145.1 9.3 reshape.479
  154.5 9.8 copy.138
  179.3 163.7 %while.87 = (s32[]{:T(128)}, f32[12,64,128]{2,1,0:T(8,128)S(1)}, s32[]{:T(128)}, f32[6,256,12,64]{1,3,2,0:T(8,128)}, pred[6,256,256,12]{2,1,3,0:T(32,128)(4,1)},...) while((s32[]{:T(128)}, f32[12,64,128]{2,1,0:T(8,128)S(1)}, ...), condition=%wide.region_6.7_spmd.clone, body=%wide.region_3.6_spmd.clone.sunk | while | flops 1318372352 | bytes 24280704 | solution.py:120
  190.3 5.8 fusion.243
  197.2 5.2 multiply_dynamic-update-slice_fusion.3
  217.6 5.8 fusion.243
  224.5 5.2 multiply_dynamic-update-slice_fusion.3
  244.7 5.8 fusion.243
  251.7 5.3 multiply_dynamic-update-slice_fusion.3
  272.1 5.7 fusion.243
  278.9 5.1 multiply_dynamic-update-slice_fusion.3
  299.1 5.8 fusion.243
  306.1 5.3 multiply_dynamic-update-slice_fusion.3
  326.5 5.8 fusion.243
  333.4 5.3 multiply_dynamic-update-slice_fusion.3
  343.0 10.7 copy.153
  353.7 10.3 reshape.474
  364.1 14.9 %multiply_reduce_fusion.8 = (f32[1536]{0:T(1024)S(1)}, f32[1536,768]{1,0:T(8,128)}, f32[1536,768]{1,0:T(8,128)}) fusion(f32[1536,768]{1,0:T(8,128)} %reshape.474, f32[1536,768]{1,0:T(8,128)} %get-tuple-element.1928, f32[768]{0:T(1024)S(1)} %mul.1119, bf16[1536,1536]{1,0:T(8,128)(2,1)} %all-gather.7.cloned.1.call-done, ...), kind=kOutput, calls=%fused_computation.205 | convolution fusion | flops 3641571840 | bytes 25961472 | tf_op jit(solution)/shard_map/dot_general | solution.py:187
  378.9 9.0 psum.84
  388.1 11.4 multiply_reduce_fusion.1
  399.5 11.8 psum.85
  411.3 13.6 %multiply_reduce_fusion.2 = (f32[768]{0:T(1024)}, f32[1536,768]{1,0:T(8,128)}, bf16[1536,768]{1,0:T(8,128)(2,1)}) fusion(f32[1536,768]{1,0:T(8,128)} %get-tuple-element.1928, f32[1536,768]{1,0:T(8,128)} %get-tuple-element.1967, f32[1536]{0:T(1024)S(1)} %psum.85, f32[1536,768]{1,0:T(8,128)} %get-tuple-element.1924, f32[1536,768]{1,0:T(8,128)} %get-tuple-element.1968, ...), kind=kLoop, calls=%fused_computation.194 | loop fusion | flops 35388672 | bytes 30692352 | tf_op jit(solution)/shard_map/reduce_sum | solution.py:229
  424.9 9.3 reshape.475
  434.2 9.8 copy.144
  448.4 234.3 %while.88 = (s32[]{:T(128)}, f32[12]{0:T(128)S(1)}, f32[12,64,128]{2,1,0:T(8,128)S(1)}, f32[6,256,12,64]{1,3,2,0:T(8,128)}, bf16[6,256,128]{2,1,0:T(8,128)(2,1)}...) while((s32[]{:T(128)}, f32[12]{0:T(128)S(1)}, ...), condition=%wide.region_23.24_spmd.clone, body=%wide.region_12.23_spmd.clone.sunk | while | flops 2628691968 | bytes 29079112 | solution.py:120
  450.2 8.7 fusion.256
  476.5 5.1 fusion.265
  489.2 8.8 fusion.256
  515.5 5.1 fusion.265
  528.2 8.7 fusion.256
  554.5 5.1 fusion.265
  567.1 8.8 fusion.256
  593.5 5.0 fusion.265
  606.1 8.7 fusion.256
  632.4 5.1 fusion.265
  645.0 8.7 fusion.256
  671.3 5.1 fusion.265
  689.6 37.1 %all-reduce.20.cloned.1.call-done = bf16[1536,256]{1,0:T(8,128)(2,1)} async-done(((bf16[1536,256]{1,0:T(8,128)(2,1)}), bf16[1536,256]{1,0:T(8,128)(2,1)}) %all-reduce.20.cloned.1.call-update) | async-done | bytes 786448 | tf_op jit(solution)/shard_map/psum | solution.py:232
  726.7 4.1 multiply_reduce_fusion.13
  734.6 10.8 copy.156
  745.4 10.1 reshape.476
  755.5 7.6 convolution_convert_fusion.3
  763.2 7.6 fusion.170
  770.8 8.3 multiply_reduce_fusion.5
  783.3 5.2 convolution_convert_fusion.2
  788.5 9.3 convolution_convert_fusion.1
  798.2 5.7 fusion.179
  804.0 6.5 fusion.180
  810.4 5.5 convolution_add_fusion.5
  821.2 8.0 convolution_convert_fusion
  835.3 13.2 %reduce-scatter.14.cloned.1.call-done = bf16[192,768]{1,0:T(8,128)(2,1)} async-done(((bf16[1536,768]{1,0:T(8,128)(2,1)}), bf16[192,768]{1,0:T(8,128)(2,1)}) %reduce-scatter.14.cloned.1.call-update) | async-done | bytes 294928 | tf_op jit(solution)/shard_map/reduce_scatter | solution.py:281
  850.3 44.3 %reduce-scatter.16.cloned.1.call-done = bf16[192,768]{1,0:T(8,128)(2,1)} async-done(((bf16[1536,768]{1,0:T(8,128)(2,1)}), bf16[192,768]{1,0:T(8,128)(2,1)}) %reduce-scatter.16.cloned.1.call-update) | async-done | bytes 294928 | tf_op jit(solution)/shard_map/reduce_scatter | solution.py:284
  896.4 44.0 %reduce-scatter.20.cloned.1.call-done = bf16[768,192]{0,1:T(8,128)(2,1)} async-done(((bf16[768,1536]{0,1:T(8,128)(2,1)}), bf16[768,192]{0,1:T(8,128)(2,1)}) %reduce-scatter.20.cloned.1.call-update) | async-done | bytes 294928 | tf_op jit(solution)/shard_map/reduce_scatter | solution.py:293
  942.2 85.7 %reduce-scatter.12.cloned.1.call-done = bf16[384,1536]{1,0:T(8,128)(2,1)} async-done(((bf16[1536,1536]{1,0:T(8,128)(2,1)}), bf16[384,1536]{1,0:T(8,128)(2,1)}) %reduce-scatter.12.cloned.1.call-update) | async-done | bytes 1179664 | tf_op jit(solution)/shard_map/reduce_scatter | solution.py:264
  1030.6 85.5 %reduce-scatter.10.cloned.1.call-done = bf16[384,1536]{1,0:T(8,128)(2,1)} async-done(((bf16[1536,1536]{1,0:T(8,128)(2,1)}), bf16[384,1536]{1,0:T(8,128)(2,1)}) %reduce-scatter.10.cloned.1.call-update) | async-done | bytes 1179664 | tf_op jit(solution)/shard_map/reduce_scatter | solution.py:216
  1116.2 4.3 fusion.151
  1120.4 131.6 %all-reduce.22.cloned.1.call-done = (f32[1536]{0:T(1024)}, f32[4,3072]{1,0:T(4,128)}, f32[3072]{0:T(1024)}, f32[4,256]{1,0:T(4,128)}, f32[256]{0:T(256)}, /*inde...) async-done(((f32[1536]{0:T(1024)}, f32[4,3072]{1,0:T(4,128)}, f32[3072]{0:T(1024)}, f32[4,256]{1,0:T(4,128)}, f32[256]{0:T(256)}, /*index=5*/f32[48]{0:T(128)}, ...) | async-done | bytes 85584 | tf_op jit(solution)/shard_map/psum | solution.py:297
  (656 shorter events, 312.7 us)
Async XLA Ops:
  7.2 7.9 copy-start.15
  7.2 18.3 %copy-start.54 = (s32[1,3]{1,0:T(1,128)S(1)}, s32[1,3]{1,0:T(1,128)}, u32[]{:S(2)}) copy-start(s32[1,3]{1,0:T(1,128)} %param.23) | copy-start | bytes 40
  7.2 18.6 %copy-start.30 = (f32[4,768]{1,0:T(4,128)S(1)}, f32[4,768]{1,0:T(4,128)}, u32[]{:S(2)}) copy-start(f32[4,768]{1,0:T(4,128)} %param.29) | copy-start | bytes 36868
  7.2 18.7 %copy-start.39 = (bf16[192,12]{0,1:T(8,128)(2,1)S(1)}, bf16[192,12]{0,1:T(8,128)(2,1)}, u32[]{:S(2)}) copy-start(bf16[192,12]{0,1:T(8,128)(2,1)} %param.28) | copy-start | bytes 13828
  7.2 28.0 %copy-start.50 = (f32[12]{0:T(128)S(1)}, f32[12]{0:T(128)}, u32[]{:S(2)}) copy-start(f32[12]{0:T(128)} %param.34) | copy-start | bytes 148
  7.2 28.0 %copy-start.42 = (f32[4,256]{1,0:T(4,128)S(1)}, f32[4,256]{1,0:T(4,128)}, u32[]{:S(2)}) copy-start(f32[4,256]{1,0:T(4,128)} %param.31) | copy-start | bytes 12292
  7.2 28.1 %copy-start.49 = (f32[12]{0:T(128)S(1)}, f32[12]{0:T(128)}, u32[]{:S(2)}) copy-start(f32[12]{0:T(128)} %param.35) | copy-start | bytes 148
  7.3 92.9 %copy-start.44 = (f32[12]{0:T(128)S(1)}, f32[12]{0:T(128)}, u32[]{:S(2)}) copy-start(f32[12]{0:T(128)} %param.33) | copy-start | bytes 148
  7.3 92.9 %all-gather.7.cloned.1.call-start = ((), (), s32[]{:S(2)}) async-start(), calls=%async_computation.7 | async-start | bytes 5898240 | tf_op jit(solution)/shard_map/all_gather | solution.py:176
  12.2 120.1 %all-gather.9.cloned.1.call-start = ((), (), s32[]{:S(2)}) async-start(), calls=%async_computation.8 | async-start | bytes 2654208 | tf_op jit(solution)/shard_map/all_gather | solution.py:181
  12.9 351.1 %all-gather.11.cloned.1.call-start = ((), (), s32[]{:S(2)}) async-start(), calls=%async_computation.9 | async-start | bytes 2654208 | tf_op jit(solution)/shard_map/all_gather | solution.py:180
  13.7 374.4 %all-gather.13.cloned.1.call-start = ((), (), s32[]{:S(2)}) async-start(), calls=%async_computation.10 | async-start | bytes 2654208 | tf_op jit(solution)/shard_map/all_gather | solution.py:214
  14.2 373.8 %all-gather.15.cloned.1.call-start = ((), (), s32[]{:S(2)}) async-start(), calls=%async_computation.12 | async-start | bytes 5898240 | tf_op jit(solution)/shard_map/all_gather | solution.py:177
  14.8 711.9 %all-reduce.20.cloned.1.call-start = ((), (), s32[]{:S(2)}) async-start(), calls=%async_computation.13 | async-start | bytes 1572864 | tf_op jit(solution)/shard_map/psum | solution.py:232
  25.5 138.8 %copy-start.6 = (bf16[1536,256]{1,0:T(8,128)(2,1)}, bf16[1536,256]{1,0:T(8,128)(2,1)S(1)}, u32[]{:S(2)}) copy-start(bf16[1536,256]{1,0:T(8,128)(2,1)S(1)} %all_gather.29) | copy-start | bytes 2359300
  25.8 112.9 %copy-start.19 = (f32[768]{0:T(1024)}, f32[768]{0:T(1024)S(1)}, u32[]{:S(2)}) copy-start(f32[768]{0:T(1024)S(1)} %get-tuple-element.1758) | copy-start | bytes 9220
  25.8 112.9 %copy-start.21 = (f32[768]{0:T(1024)}, f32[768]{0:T(1024)S(1)}, u32[]{:S(2)}) copy-start(f32[768]{0:T(1024)S(1)} %get-tuple-element.1759) | copy-start | bytes 9220
  25.9 112.9 %copy-start.23 = (f32[768]{0:T(1024)}, f32[768]{0:T(1024)S(1)}, u32[]{:S(2)}) copy-start(f32[768]{0:T(1024)S(1)} %get-tuple-element.1760) | copy-start | bytes 9220
  25.9 112.9 %copy-start.25 = (f32[768]{0:T(1024)}, f32[768]{0:T(1024)S(1)}, u32[]{:S(2)}) copy-start(f32[768]{0:T(1024)S(1)} %get-tuple-element.1761) | copy-start | bytes 9220
  35.3 103.4 %copy-start.12 = (bf16[1536,12]{0,1:T(8,128)(2,1)}, bf16[1536,12]{0,1:T(8,128)(2,1)S(1)}, u32[]{:S(2)}) copy-start(bf16[1536,12]{0,1:T(8,128)(2,1)S(1)} %reshape.457) | copy-start | bytes 110596
  35.3 132.8 %copy-start.31 = (f32[1,256]{1,0:T(1,128)}, f32[1,256]{1,0:T(1,128)S(1)}, u32[]{:S(2)}) copy-start(f32[1,256]{1,0:T(1,128)S(1)} %get-tuple-element.1961) | copy-start | bytes 3076
  35.3 132.8 %copy-start.33 = (f32[1,256]{1,0:T(1,128)}, f32[1,256]{1,0:T(1,128)S(1)}, u32[]{:S(2)}) copy-start(f32[1,256]{1,0:T(1,128)S(1)} %get-tuple-element.1962) | copy-start | bytes 3076
  35.3 132.8 %copy-start.35 = (f32[1,256]{1,0:T(1,128)}, f32[1,256]{1,0:T(1,128)S(1)}, u32[]{:S(2)}) copy-start(f32[1,256]{1,0:T(1,128)S(1)} %get-tuple-element.1963) | copy-start | bytes 3076
  35.3 132.8 %copy-start.37 = (f32[1,256]{1,0:T(1,128)}, f32[1,256]{1,0:T(1,128)S(1)}, u32[]{:S(2)}) copy-start(f32[1,256]{1,0:T(1,128)S(1)} %get-tuple-element.1964) | copy-start | bytes 3076
  104.5 34.2 %copy-start.40 = (f32[768]{0:T(1024)S(1)}, f32[768]{0:T(1024)}, u32[]{:S(2)}) copy-start(f32[768]{0:T(1024)} %param.30) | copy-start | bytes 9220
  138.7 6.5 copy-start
  164.3 3.8 copy-start.45
  168.1 2.8 copy-start.1
  364.1 24.0 %copy-start.41 = (f32[768]{0:T(1024)S(1)}, f32[768]{0:T(1024)}, u32[]{:S(2)}) copy-start(f32[768]{0:T(1024)} %param.36) | copy-start | bytes 9220
  448.4 236.9 %copy-start.11 = (f32[1536,12]{0,1:T(8,128)S(1)}, f32[1536,12]{0,1:T(8,128)}, u32[]{:S(2)}) copy-start(f32[1536,12]{0,1:T(8,128)} %get-tuple-element.1966) | copy-start | bytes 221188
  682.7 44.0 %copy-start.2 = (f32[1536,256]{1,0:T(8,128)S(1)}, f32[1536,256]{1,0:T(8,128)}, u32[]{:S(2)}) copy-start(f32[1536,256]{1,0:T(8,128)} %copy-done.1) | copy-start | bytes 4718596
  682.7 44.0 %copy-start.4 = (f32[1536,256]{1,0:T(8,128)S(1)}, f32[1536,256]{1,0:T(8,128)}, u32[]{:S(2)}) copy-start(f32[1536,256]{1,0:T(8,128)} %get-tuple-element.1926) | copy-start | bytes 4718596
  685.0 146.6 %reduce-scatter.22.cloned.1.call-start = ((), (), s32[]{:S(2)}) async-start(), calls=%async_computation.19 | async-start | bytes 442368
  689.5 144.2 %reduce-scatter.18.cloned.1.call-start = ((), (), s32[]{:S(2)}) async-start(), calls=%async_computation.17 | async-start | bytes 884736 | tf_op jit(solution)/shard_map/reduce_scatter | solution.py:287
  726.7 5.4 slice-start
  730.8 0.9 copy-start.38
  730.8 1.4 slice-start.1
  734.6 113.9 %reduce-scatter.14.cloned.1.call-start = ((), (), s32[]{:S(2)}) async-start(), calls=%async_computation.15 | async-start | bytes 2654208 | tf_op jit(solution)/shard_map/reduce_scatter | solution.py:281
  745.4 10.1 copy-start.8
  763.1 131.4 %reduce-scatter.16.cloned.1.call-start = ((), (), s32[]{:S(2)}) async-start(), calls=%async_computation.16 | async-start | bytes 2654208 | tf_op jit(solution)/shard_map/reduce_scatter | solution.py:284
  779.8 3.5 slice-start.2
  780.5 2.8 slice-start.3
  781.9 1.4 copy-start.9
  788.5 151.9 %reduce-scatter.20.cloned.1.call-start = ((), (), s32[]{:S(2)}) async-start(), calls=%async_computation.18 | async-start | bytes 2654208 | tf_op jit(solution)/shard_map/reduce_scatter | solution.py:293
  797.9 230.0 %reduce-scatter.12.cloned.1.call-start = ((), (), s32[]{:S(2)}) async-start(), calls=%async_computation.14 | async-start | bytes 5898240 | tf_op jit(solution)/shard_map/reduce_scatter | solution.py:264
  798.2 5.8 copy-start.10
  798.2 5.8 copy-start.53
  803.9 6.5 copy-start.7
  810.4 5.5 copy-start.13
  819.5 1.7 copy-start.52
  819.6 296.6 %reduce-scatter.10.cloned.1.call-start = ((), (), s32[]{:S(2)}) async-start(), calls=%async_computation.11 | async-start | bytes 5898240 | tf_op jit(solution)/shard_map/reduce_scatter | solution.py:216
  829.2 1.6 copy-start.43
  829.2 2.0 copy-start.51
  829.2 198.8 %copy-start.3 = (bf16[384,1536]{1,0:T(8,128)(2,1)S(1)}, bf16[384,1536]{1,0:T(8,128)(2,1)}, u32[]{:S(2)}) copy-start(bf16[384,1536]{1,0:T(8,128)(2,1)} %param.21) | copy-start | bytes 3538948
  829.2 198.8 %copy-start.16 = (f32[1536]{0:T(1024)S(1)}, f32[1536]{0:T(1024)}, u32[]{:S(2)}) copy-start(f32[1536]{0:T(1024)} %param.24) | copy-start | bytes 18436
  829.2 198.7 %copy-start.28 = (f32[384]{0:T(512)S(1)}, f32[384]{0:T(512)}, u32[]{:S(2)}) copy-start(f32[384]{0:T(512)} %copy-done.27) | copy-start | bytes 4612
  829.2 286.9 %copy-start.5 = (bf16[384,1536]{1,0:T(8,128)(2,1)S(1)}, bf16[384,1536]{1,0:T(8,128)(2,1)}, u32[]{:S(2)}) copy-start(bf16[384,1536]{1,0:T(8,128)(2,1)} %param.22) | copy-start | bytes 3538948
  829.3 422.8 %all-reduce.22.cloned.1.call-start = ((), (), s32[]{:S(2)}) async-start(), calls=%async_computation.20 | async-start | bytes 177152 | tf_op jit(solution)/shard_map/psum | solution.py:297
  830.3 200.2 %copy-start.47 = (f32[48]{0:T(128)}, f32[48]{0:T(128)S(1)}, u32[]{:S(2)}) copy-start(f32[48]{0:T(128)S(1)} %dynamic_update_slice.232) | copy-start | bytes 580
  830.5 200.0 %copy-start.48 = (f32[48]{0:T(128)}, f32[48]{0:T(128)S(1)}, u32[]{:S(2)}) copy-start(f32[48]{0:T(128)S(1)} %dynamic_update_slice.234) | copy-start | bytes 580
  830.8 199.7 %copy-start.17 = (f32[3072]{0:T(1024)}, f32[3072]{0:T(1024)S(1)}, u32[]{:S(2)}) copy-start(f32[3072]{0:T(1024)S(1)} %dynamic_update_slice.231) | copy-start | bytes 36868
  831.1 199.4 %copy-start.18 = (f32[3072]{0:T(1024)}, f32[3072]{0:T(1024)S(1)}, u32[]{:S(2)}) copy-start(f32[3072]{0:T(1024)S(1)} %dynamic_update_slice.235) | copy-start | bytes 36868
  831.2 199.4 %copy-start.14 = (f32[4,3072]{1,0:T(4,128)}, f32[4,3072]{1,0:T(4,128)S(1)}, u32[]{:S(2)}) copy-start(f32[4,3072]{1,0:T(4,128)S(1)} %maximum_dynamic-update-slice_fusion) | copy-start | bytes 147460
  831.5 199.1 %copy-start.46 = (f32[48]{0:T(128)}, f32[48]{0:T(128)S(1)}, u32[]{:S(2)}) copy-start(f32[48]{0:T(128)S(1)} %multiply_dynamic-update-slice_fusion.1) | copy-start | bytes 580
  (9 other events, 6.6 us)
Sparse Core Ops, SparseCore 0:
  12.3 87.8 all-gather.6
  102.0 30.2 all-gather.8
  134.2 29.0 all-gather.10
  165.0 29.0 all-gather.12
  195.5 86.6 all-gather.14
  685.1 41.5 all-reduce.19
  730.3 33.4 reduce-scatter.21
  767.6 34.9 reduce-scatter.17
  806.0 42.4 reduce-scatter.13
  852.1 42.4 reduce-scatter.15
  897.9 42.4 reduce-scatter.19
  942.7 85.2 reduce-scatter.11
  1030.4 85.7 reduce-scatter.9
  1124.7 127.2 all-reduce.21
where the time goes:
time: 1280 us; the launch traced here: 1270 us
  waiting for transfers between devices  537 us (42%)
  matrix products  318 us (25%)
  other arithmetic  190 us (15%)
  local copies, waits for them, and re-layouts  159 us (12%)
  blocking collectives  40.5 us (3%)
  between operations  15.3 us (1%)
    psum x1, waiting for transfers between devices, local(): lax.psum((grad_norm_gain, widen(grad_conv_x, parts, position, 1), widen(g...  132 us
    dot_general x18, matrix products, block_step(): local_part = jnp.einsum('tsh,shp->thp', mixing, x_block, precision=highest)  118 us
    reduce_scatter x1, waiting for transfers between devices, local(): lax.psum_scatter(contribution.astype(jnp.bfloat16), 'tensor', scatter_dim...  85.7 us
    reduce_scatter x1, waiting for transfers between devices, local(): lax.psum_scatter(branch_part.astype(jnp.bfloat16), 'tensor', scatter_dime...  85.5 us
    all_gather x1, waiting for transfers between devices, local(): lax.all_gather(normed, 'tensor', axis=0, tiled=True)  64.6 us
    dynamic_update_slice x42, other arithmetic, run_scan(): _, ys = lax.scan(partial(block_step, rate), begin, pieces)  60.7 us
    reduce_scatter x1, waiting for transfers between devices, local(): lax.psum_scatter(grad_w_x.astype(jnp.bfloat16), 'dp', scatter_dimension=0...  44.3 us
    reduce_scatter x1, waiting for transfers between devices, local(): lax.psum_scatter(grad_w_out.astype(jnp.bfloat16), 'dp', scatter_dimension...  44 us
  transfers between devices with their start and end apart: 14, of which 9 were waited for; matrix products, arithmetic and copies ran while one was open for 29% of the time, Pallas kernels for 0%

commit v1 on v0

v1 whole, which is shorter than its diff:
```python
from functools import partial

import jax
import jax.numpy as jnp
from jax import lax
from jax.experimental import pallas as pl
from jax.experimental.pallas import tpu as pltpu
from jax.sharding import PartitionSpec as P

SPAN = 256
HALO = 16
LANES = 128
LOG2E = 1.4426950408889634
EPS = 1e-05
FAR = -1e30
HIGH = lax.Precision.HIGHEST
F32 = jnp.float32
BF16 = jnp.bfloat16
VMEM_BYTES = 60 * 1024 * 1024


def nn(a, b):
    return jnp.dot(a, b, preferred_element_type=F32)


def nt(a, b):
    return lax.dot_general(a, b, (((1,), (1,)), ((), ())), preferred_element_type=F32)


def tn(a, b):
    return lax.dot_general(a, b, (((0,), (0,)), ((), ())), preferred_element_type=F32)


def sigmoid(v):
    return 1.0 / (1.0 + jnp.exp(-v))


def iota(shape, axis):
    return lax.broadcasted_iota(jnp.int32, shape, axis)


def seg_at(sc, pos):
    found = (pos >= sc[0]).astype(jnp.int32)
    for i in range(1, 3):
        found = found + (pos >= sc[i]).astype(jnp.int32)
    return jnp.where(pos < 0, -1, found)


def same_as_behind(sc, pos, offset):
    return (seg_at(sc, pos - offset) == seg_at(sc, pos)).astype(F32)


def head_map(cols, start, dtype=BF16, both=True):
    k = iota((LANES, cols), 0)
    if both:
        k = k & 63
    head = (iota((LANES, cols), 1) + start) >> 6
    return (k == head).astype(dtype)


def expand(values, mapping):
    high = values.astype(BF16).astype(F32)
    low = values - high
    return nn((high + pltpu.roll(low, 64, axis=1)).astype(BF16), mapping)


def assemble(me, rows, parts, refs, scratch):
    for (order, low), ref in zip(parts, refs):
        for i, v in enumerate(order):
            start = pl.multiple_of((me ^ v) * rows, 16)
            scratch[pl.ds(start, rows), low : low + ref.shape[2]] = ref[i]


def whole():
    return pl.BlockSpec(memory_space=pltpu.VMEM)


def scalars():
    return pl.BlockSpec(memory_space=pltpu.SMEM)


def params():
    return pltpu.CompilerParams(vmem_limit_bytes=VMEM_BYTES)


def cost(flops, nbytes):
    return pl.CostEstimate(flops=int(flops), bytes_accessed=int(nbytes), transcendentals=0)


def maps_body(parts, rows, ha, sc, tok, taps, bias, dtb, alog, *rest):
    n = len(parts)
    refs, outs = rest[:n], rest[n : n + 9]
    wscr = rest[n + 9]
    pre_o, bc_o, dtin_o, dt_o, lc_o, lr_o, em_o, et_o, kd_o = outs
    count = bc_o.shape[0]
    chunks = count // SPAN
    assemble(sc[4], rows, parts, refs, wscr)
    pre_o[...] = nn(tok[...], wscr[:, LANES:])
    base = sc[3]
    pos = base + iota((count, 1), 0)
    acc = bias[...] + taps[0:1, :] * pre_o[HALO : HALO + count, :]
    for j in range(1, 4):
        acc = acc + taps[j : j + 1, :] * pre_o[HALO - j : HALO - j + count, :] * same_as_behind(sc, pos, j)
    bc_o[...] = (acc * sigmoid(acc)).astype(BF16)
    dtin = nn(tok[HALO:, :], wscr[:, :LANES]) + dtb[...]
    steps = jnp.maximum(dtin, 0.0) + jnp.log1p(jnp.exp(-jnp.abs(dtin)))
    scaled = steps * (-jnp.exp(alog[...]) * LOG2E)
    lane = iota((1, LANES), 1)
    keep = (lane < ha).astype(F32)

    def block(v, b):
        if b:
            v = pltpu.roll(v, LANES - ha, axis=1)
        return v * keep

    for b in range(2):
        dtin_o[b] = block(dtin, b)
        dt_o[b] = block(steps, b)
    tri = (iota((SPAN, SPAN), 0) >= iota((SPAN, SPAN), 1)).astype(F32)
    gone = []
    for c in range(chunks):
        span = slice(c * SPAN, (c + 1) * SPAN)
        logs = jnp.dot(tri, scaled[span, :], precision=HIGH, preferred_element_type=F32)
        first, last = base + c * SPAN - 1, base + (c + 1) * SPAN - 1
        here = base + c * SPAN + iota((SPAN, 1), 0)
        seg = seg_at(sc, here)
        seg_first, seg_last = seg_at(sc, first), seg_at(sc, last)
        starts = (seg == seg_first).astype(F32)
        ends = (seg == seg_last).astype(F32)
        final = logs[SPAN - 1 : SPAN, :]
        lead = starts * jnp.exp2(logs)
        tail = ends * jnp.exp2(final - logs)
        kept = jnp.where(seg_first == seg_last, 1.0, 0.0).astype(F32)
        gone.append(kept * jnp.exp2(final))
        for b in range(2):
            mine = block(logs, b)
            lc_o[b, span, :] = mine
            lr_o[b, :, span] = mine.T[:16, :]
            em_o[b, span, :] = block(lead, b)
            et_o[b, span, :] = block(tail, b)
    ones = jnp.ones((1, LANES), F32)
    ahead_of, behind_of = [ones], [ones]
    for c in range(chunks - 1):
        ahead_of.append(ahead_of[-1] * gone[c])
        behind_of.append(behind_of[-1] * gone[chunks - 1 - c])
    behind_of = behind_of[::-1]
    fill = [jnp.zeros((1, LANES), F32)] * (8 - chunks)
    table = jnp.concatenate(gone + fill + ahead_of + fill + behind_of + fill, axis=0)
    for b in range(2):
        kd_o[b] = block(table, b)


def run_maps(sc, tok, taps, bias, dtb, alog, pieces, rows, ha):
    parts, refs = pieces
    total, width = tok.shape
    count = total - HALO
    small = sum(r.shape[2] for r, p in zip(refs, parts) if p[0][0] == 0)
    per_block = jax.ShapeDtypeStruct((2, count, LANES), F32)
    return pl.pallas_call(
        partial(maps_body, parts, rows, ha),
        out_shape=(
            jax.ShapeDtypeStruct((total, 2 * LANES), F32),
            jax.ShapeDtypeStruct((count, 2 * LANES), BF16),
            per_block,
            per_block,
            per_block,
            jax.ShapeDtypeStruct((2, 16, count), F32),
            per_block,
            per_block,
            jax.ShapeDtypeStruct((2, 24, LANES), F32),
        ),
        in_specs=[scalars()] + [whole()] * (5 + len(refs)),
        out_specs=[whole()] * 9,
        scratch_shapes=[pltpu.VMEM((width, small), BF16)],
        compiler_params=params(),
        cost_estimate=cost(2 * total * width * 512, 8e6),
        name="maps",
    )(sc, tok, taps, bias, dtb, alog, *refs)


def xpath_body(parts, rows, ig, sc, tok, taps, bias, bc, dt, et, kd, *rest):
    n = len(parts)
    refs = rest[:n]
    pre_o, xs_o, st_o, fin_o, wscr = rest[n:]
    count, cols = xs_o.shape
    j = pl.program_id(0)

    @pl.when(j == 0)
    def _():
        assemble(sc[4], rows, parts, refs, wscr)

    at = pl.multiple_of(j * cols, cols)
    pre_o[...] = nn(tok[...], wscr[:, pl.ds(at, cols)])
    mapping = head_map(cols, lax.rem(at, ig))
    state = jnp.zeros((LANES, cols), F32)
    gone = expand(kd[0], mapping)
    for c in range(count // SPAN):
        low = c * SPAN
        pos = sc[3] + low + iota((SPAN, 1), 0)
        acc = bias[...] + taps[0:1, :] * pre_o[HALO + low : HALO + low + SPAN, :]
        for k in range(1, 4):
            acc = acc + taps[k : k + 1, :] * pre_o[HALO + low - k : HALO + low - k + SPAN, :] * same_as_behind(sc, pos, k)
        xs = (acc * sigmoid(acc)).astype(BF16)
        xs_o[low : low + SPAN, :] = xs
        weight = expand(dt[0, low : low + SPAN, :] * et[0, low : low + SPAN, :], mapping)
        st_o[c] = state
        state = gone[c : c + 1, :] * state + tn(bc[low : low + SPAN, :LANES], (xs.astype(F32) * weight).astype(BF16))
    fin_o[...] = state.astype(BF16)


def col_tile(ig):
    return 256 if ig % 256 == 0 else 128


def run_xpath(sc, tok, taps, bias, bc, dt, et, kd, pieces, rows, ig):
    parts, refs = pieces
    total, width = tok.shape
    count = total - HALO
    inner = 2 * ig
    cols = col_tile(ig)
    chunks = count // SPAN
    per_block = pl.BlockSpec((1, count, LANES), lambda j: (j * cols // ig, 0, 0))
    return pl.pallas_call(
        partial(xpath_body, parts, rows, ig),
        grid=(inner // cols,),
        out_shape=(
            jax.ShapeDtypeStruct((total, inner), F32),
            jax.ShapeDtypeStruct((count, inner), BF16),
            jax.ShapeDtypeStruct((chunks, LANES, inner), F32),
            jax.ShapeDtypeStruct((LANES, inner), BF16),
        ),
        in_specs=[
            scalars(),
            whole(),
            pl.BlockSpec((4, cols), lambda j: (0, j)),
            pl.BlockSpec((1, cols), lambda j: (0, j)),
            whole(),
            per_block,
            per_block,
            pl.BlockSpec((1, 24, LANES), lambda j: (j * cols // ig, 0, 0)),
        ]
        + [whole()] * len(refs),
        out_specs=(
            pl.BlockSpec((total, cols), lambda j: (0, j)),
            pl.BlockSpec((count, cols), lambda j: (0, j)),
            pl.BlockSpec((chunks, LANES, cols), lambda j: (0, 0, j)),
            pl.BlockSpec((LANES, cols), lambda j: (0, j)),
        ),
        scratch_shapes=[pltpu.VMEM((width, inner), BF16)],
        compiler_params=params(),
        cost_estimate=cost(2.4 * total * width * inner, 20e6),
        name="xpath",
    )(sc, tok, taps, bias, bc, dt, et, kd, *refs)


def proj_body(parts, rows, sc, x, *rest):
    n = len(parts)
    out, wscr = rest[n:]
    cols = out.shape[1]
    j = pl.program_id(0)

    @pl.when(j == 0)
    def _():
        assemble(sc[4], rows, parts, rest[:n], wscr)

    skip = x.shape[0] - out.shape[0]
    out[...] = nn(x[skip:, :], wscr[:, pl.ds(pl.multiple_of(j * cols, cols), cols)])


def run_proj(sc, x, pieces, rows, inner, count):
    parts, refs = pieces
    width = x.shape[1]
    cols = 256
    return pl.pallas_call(
        partial(proj_body, parts, rows),
        grid=(inner // cols,),
        out_shape=jax.ShapeDtypeStruct((count, inner), F32),
        in_specs=[scalars()] + [whole()] * (1 + len(refs)),
        out_specs=pl.BlockSpec((count, cols), lambda j: (0, j)),
        scratch_shapes=[pltpu.VMEM((width, inner), BF16)],
        compiler_params=params(),
        cost_estimate=cost(2 * count * width * inner, 12e6),
        name="proj",
    )(sc, x, *refs)


def back_body(parts, rows, sc, x, *rest):
    n = len(parts)
    out, wscr = rest[n:]
    cols = out.shape[1]
    j = pl.program_id(0)

    @pl.when(j == 0)
    def _():
        assemble(sc[4], rows, parts, rest[:n], wscr)

    out[...] = nt(x[...], wscr[pl.ds(pl.multiple_of(j * cols, cols), cols), :]).astype(BF16)


def run_back(sc, x, pieces, rows, width):
    parts, refs = pieces
    count, inner = x.shape
    cols = 256
    return pl.pallas_call(
        partial(back_body, parts, rows),
        grid=(width // cols,),
        out_shape=jax.ShapeDtypeStruct((count, width), BF16),
        in_specs=[scalars()] + [whole()] * (1 + len(refs)),
        out_specs=pl.BlockSpec((count, cols), lambda j: (0, j)),
        scratch_shapes=[pltpu.VMEM((width, inner), BF16)],
        compiler_params=params(),
        cost_estimate=cost(2 * count * width * inner, 10e6),
        name="back",
    )(sc, x, *refs)


def grad_body(rows, sc, x, y, own, oth, scr):
    skip = x.shape[0] - y.shape[0]
    scr[...] = tn(x[skip:, :], y[...]).astype(BF16)
    me = sc[4]
    for v in range(2 * own.shape[0]):
        block = scr[pl.ds(pl.multiple_of((me ^ v) * rows, 16), rows), :]
        if v & 1:
            oth[v >> 1] = block
        else:
            own[v >> 1] = block


def run_grad(sc, x, y, rows):
    width = x.shape[1]
    count, inner = y.shape
    cols = 256 if inner % 256 == 0 else 128
    half = width // rows // 2
    shape = jax.ShapeDtypeStruct((half, rows, inner), BF16)
    spec = pl.BlockSpec((half, rows, cols), lambda j: (0, 0, j))
    return pl.pallas_call(
        partial(grad_body, rows),
        grid=(inner // cols,),
        out_shape=(shape, shape),
        in_specs=[scalars(), whole(), pl.BlockSpec((count, cols), lambda j: (0, j))],
        out_specs=(spec, spec),
        scratch_shapes=[pltpu.VMEM((width, cols), BF16)],
        compiler_params=params(),
        cost_estimate=cost(2 * count * width * inner, 10e6),
        name="grad",
    )(sc, x, y)


def scan_body(sc, xs, bc, dt, lc, lr, em, kd, st, sin, z, dm, skip, gain, y_o, stat_o, cb, off):
    c, b = pl.program_id(0), pl.program_id(1)
    cols = xs.shape[1]

    @pl.when(b == 0)
    def _():
        cb[...] = nt(bc[:, LANES:], bc[:, :LANES])
        start = sc[3] + c * SPAN
        t, s = iota((SPAN, SPAN), 0), iota((SPAN, SPAN), 1)
        seen = (t >= s) & (seg_at(sc, start + t) == seg_at(sc, start + s))
        off[...] = jnp.where(seen, 0.0, FAR)
        stat_o[...] = jnp.zeros_like(stat_o)

    mapping = head_map(cols, 0)
    scaled = (xs[...].astype(F32) * expand(dt[0], mapping)).astype(BF16)
    carry = expand(kd[0, 8:16, :], mapping)
    rows8 = (iota((8, 1), 0) == c).astype(F32)
    state = st[0] + jnp.sum(carry * rows8, axis=0, keepdims=True) * sin[...].astype(F32)
    far = nn(bc[:, LANES:], state.astype(BF16)) * expand(em[0], mapping) + skip[...] * xs[...].astype(F32)
    lane = iota((1, LANES), 1)
    sides = [(lane < 64).astype(BF16), (lane >= 64).astype(BF16)]
    half = SPAN // 2
    square = jnp.zeros((SPAN, 1), F32)
    cross = jnp.zeros((SPAN, 1), F32)
    for k in range(cols // LANES):
        at = slice(k * LANES, (k + 1) * LANES)
        pair = scaled[:, at]
        top = far[:half, at]
        low = far[half:, at]
        for side in range(2):
            h = 2 * k + side
            operand = pair * sides[side]
            column = lc[0, :, h : h + 1]
            row = lr[0, h : h + 1, :]
            w_top = cb[:half, :half] * jnp.exp2(column[:half] - row[:, :half] + off[:half, :half])
            top = top + nn(w_top.astype(BF16), operand[:half, :])
            w_low = cb[half:, :] * jnp.exp2(column[half:] - row + off[half:, :])
            low = low + nn(w_low.astype(BF16), operand)
        out = jnp.concatenate([top, low], axis=0)
        y_o[:, at] = out
        gate = z[:, at]
        gated = out * (gate * sigmoid(gate))
        square = square + jnp.sum(gated * gated, axis=1, keepdims=True)
        cross = cross + jnp.sum(gated * (dm[:, at] * gain[:, at]), axis=1, keepdims=True)
    stat_o[...] += jnp.where(lane == 0, square, 0.0) + jnp.where(lane == 1, cross, 0.0)


def run_scan(sc, xs, bc, dt, lc, lr, em, kd, st, sin, z, dm, skip, gain, ig):
    count, inner = xs.shape
    chunks = count // SPAN
    tile = pl.BlockSpec((SPAN, ig), lambda c, b: (c, b))
    per_block = pl.BlockSpec((1, SPAN, LANES), lambda c, b: (b, c, 0))
    row = pl.BlockSpec((1, ig), lambda c, b: (0, b))
    return pl.pallas_call(
        scan_body,
        grid=(chunks, 2),
        out_shape=(
            jax.ShapeDtypeStruct((count, inner), F32),
            jax.ShapeDtypeStruct((count, LANES), F32),
        ),
        in_specs=[
            scalars(),
            tile,
            pl.BlockSpec((SPAN, 2 * LANES), lambda c, b: (c, 0)),
            per_block,
            per_block,
            pl.BlockSpec((1, 16, SPAN), lambda c, b: (b, 0, c)),
            per_block,
            pl.BlockSpec((1, 24, LANES), lambda c, b: (b, 0, 0)),
            pl.BlockSpec((1, LANES, ig), lambda c, b: (c, 0, b)),
            pl.BlockSpec((LANES, ig), lambda c, b: (0, b)),
            tile,
            tile,
            row,
            row,
        ],
        out_specs=(tile, pl.BlockSpec((SPAN, LANES), lambda c, b: (c, 0))),
        scratch_shapes=[pltpu.VMEM((SPAN, SPAN), F32), pltpu.VMEM((SPAN, SPAN), F32)],
        compiler_params=params(),
        cost_estimate=cost(6e9, 20e6),
        name="scan",
    )(sc, xs, bc, dt, lc, lr, em, kd, st, sin, z, dm, skip, gain)


def gate_body(ig, inner_all, sc, y, z, dm, stat_a, stat_b, xs, gain, bc, em, kd, mixed_o, dz_o, dy_o, sums_o, ds_o, first_o):
    count, cols = y.shape
    at = pl.program_id(0) * cols
    mapping = head_map(cols, lax.rem(at, ig))
    gone = expand(kd[0], mapping)
    grad = jnp.zeros((LANES, cols), F32)
    by_gain = jnp.zeros((1, cols), F32)
    by_skip = jnp.zeros((1, cols), F32)
    for c in range(count // SPAN - 1, -1, -1):
        span = slice(c * SPAN, (c + 1) * SPAN)
        stat = stat_a[span, :] + stat_b[span, :]
        scale = lax.rsqrt(stat[:, 0:1] / inner_all + EPS)
        pull = scale * scale * scale * stat[:, 1:2] / inner_all
        gate = z[span, :]
        sig = sigmoid(gate)
        act = gate * sig
        out = y[span, :]
        gated = out * act
        normal = gated * scale
        mixed_o[span, :] = (normal * gain[...]).astype(BF16)
        upstream = dm[span, :]
        by_gain = by_gain + jnp.sum(upstream * normal, axis=0, keepdims=True)
        dgated = scale * (upstream * gain[...]) - gated * pull
        dz_o[span, :] = (dgated * out * (sig * (1.0 + gate * (1.0 - sig)))).astype(BF16)
        dy = dgated * act
        by_skip = by_skip + jnp.sum(dy * xs[span, :].astype(F32), axis=0, keepdims=True)
        dy_o[span, :] = dy.astype(BF16)
        ds_o[c] = grad
        lead = (dy * expand(em[0, span, :], mapping)).astype(BF16)
        grad = gone[c : c + 1, :] * grad + tn(bc[span, LANES:], lead)
    first_o[...] = grad.astype(BF16)
    sums_o[...] = jnp.concatenate([by_gain, by_skip, jnp.zeros((6, cols), F32)], axis=0)


def run_gate(sc, y, z, dm, stat_a, stat_b, xs, gain, bc, em, kd, ig, inner_all):
    count, inner = y.shape
    cols = col_tile(ig)
    chunks = count // SPAN
    tile = pl.BlockSpec((count, cols), lambda j: (0, j))
    low = jax.ShapeDtypeStruct((count, inner), BF16)
    return pl.pallas_call(
        partial(gate_body, ig, inner_all),
        grid=(inner // cols,),
        out_shape=(
            low,
            low,
            low,
            jax.ShapeDtypeStruct((8, inner), F32),
            jax.ShapeDtypeStruct((chunks, LANES, inner), F32),
            jax.ShapeDtypeStruct((LANES, inner), BF16),
        ),
        in_specs=[
            scalars(),
            tile,
            tile,
            tile,
            whole(),
            whole(),
            tile,
            pl.BlockSpec((1, cols), lambda j: (0, j)),
            whole(),
            pl.BlockSpec((1, count, LANES), lambda j: (j * cols // ig, 0, 0)),
            pl.BlockSpec((1, 24, LANES), lambda j: (j * cols // ig, 0, 0)),
        ],
        out_specs=(
            tile,
            tile,
            tile,
            pl.BlockSpec((8, cols), lambda j: (0, j)),
            pl.BlockSpec((chunks, LANES, cols), lambda j: (0, 0, j)),
            pl.BlockSpec((LANES, cols), lambda j: (0, j)),
        ),
        compiler_params=params(),
        cost_estimate=cost(4e9, 30e6),
        name="gate",
    )(sc, y, z, dm, stat_a, stat_b, xs, gain, bc, em, kd)


def pull_body(
    ha, sc, xs, dy, bc, dtin, dt, lc, lr, em, et, kd, st, sin, ds, dsin, pre, taps, bias, skip, alog,
    dx_o, dbc_o, ddt_o, csum_o, hsum_o, cbt, off, dcb, ahead, dxi, rsum,
):
    b, step = pl.program_id(0), pl.program_id(1)
    chunks = pl.num_programs(1)
    c = chunks - 1 - step
    cols = xs.shape[1]
    half = SPAN // 2
    start = sc[3] + c * SPAN
    b_map, c_map = bc[:, :LANES], bc[:, LANES:]
    cbt[...] = nt(b_map, c_map)
    s, t = iota((SPAN, SPAN), 0), iota((SPAN, SPAN), 1)
    seen = (t >= s) & (seg_at(sc, start + t) == seg_at(sc, start + s))
    off[...] = jnp.where(seen, 0.0, FAR)
    dcb[...] = jnp.zeros_like(dcb)

    @pl.when(step == 0)
    def _():
        ahead[...] = jnp.zeros_like(ahead)
        csum_o[...] = jnp.zeros_like(csum_o)
        hsum_o[...] = jnp.zeros_like(hsum_o)
        rsum[...] = jnp.zeros_like(rsum)

    mapping = head_map(cols, 0)
    single = head_map(cols, 0, both=False)
    lane = iota((1, LANES), 1)
    sides = [(lane < 64).astype(BF16), (lane >= 64).astype(BF16)]
    steps = dt[0]
    steps_wide = expand(steps, mapping)
    xf = xs[...].astype(F32)
    scaled = (xf * steps_wide).astype(BF16)
    dyl = dy[...]
    csums = jnp.zeros((SPAN, LANES), F32)
    for k in range(cols // LANES):
        at = slice(k * LANES, (k + 1) * LANES)
        x_pair, dy_pair = scaled[:, at], dyl[:, at]
        top = jnp.zeros((half, LANES), F32)
        low = jnp.zeros((half, LANES), F32)
        for side in range(2):
            h = 2 * k + side
            x_one = x_pair * sides[side]
            dy_one = dy_pair * sides[side]
            column = lc[0, :, h : h + 1]
            row = lr[0, h : h + 1, :]
            decay = jnp.exp2(row - column[:half] + off[:half, :])
            top = top + nn((cbt[:half, :] * decay).astype(BF16), dy_one)
            share = nt(x_one[:half, :], dy_pair) * decay
            dcb[:half, :] += share
            both = share * cbt[:half, :]
            row_sum = jnp.sum(both, axis=0, keepdims=True)
            col_top = jnp.sum(both, axis=1, keepdims=True)
            decay = jnp.exp2(row[:, half:] - column[half:] + off[half:, half:])
            low = low + nn((cbt[half:, half:] * decay).astype(BF16), dy_one[half:, :])
            share = nt(x_one[half:, :], dy_pair[half:, :]) * decay
            dcb[half:, half:] += share
            both = share * cbt[half:, half:]
            rsum[h : h + 1, :half] = row_sum[:, :half]
            rsum[h : h + 1, half:] = row_sum[:, half:] + jnp.sum(both, axis=0, keepdims=True)
            col_low = jnp.sum(both, axis=1, keepdims=True)
            csums = csums + jnp.where(lane == h, jnp.concatenate([col_top, col_low], axis=0), 0.0)
        dxi[:half, at] = top
        dxi[half:, at] = low
    lead_wide = expand(em[0], mapping)
    tail_wide = expand(et[0], mapping)
    decays = expand(kd[0], mapping)
    pick = (iota((8, 1), 0) == c).astype(F32)
    state = st[0] + jnp.sum(decays[8:16] * pick, axis=0, keepdims=True) * sin[...].astype(F32)
    dstate = ds[0] + jnp.sum(decays[16:24] * pick, axis=0, keepdims=True) * dsin[...].astype(F32)
    state_l, dstate_l = state.astype(BF16), dstate.astype(BF16)
    dyf = dyl.astype(F32)
    led = dyf * lead_wide
    read = nn(c_map, state_l)
    dx_far = nn(b_map, dstate_l) * tail_wide
    db = nn(dcb[...].astype(BF16), c_map) + nt((scaled.astype(F32) * tail_wide).astype(BF16), dstate_l)
    dc = tn(dcb[...].astype(BF16), b_map) + nt(led.astype(BF16), state_l)
    rows_here = pl.ds(pl.multiple_of(c * SPAN, SPAN), SPAN)

    @pl.when(b == 0)
    def _():
        dbc_o[rows_here, :LANES] = db
        dbc_o[rows_here, LANES:] = dc

    @pl.when(b > 0)
    def _():
        dbc_o[rows_here, :LANES] += db
        dbc_o[rows_here, LANES:] += dc

    near = dxi[...]
    from_near = nt((xf * near).astype(BF16), single)
    from_far = nt((xf * dx_far).astype(BF16), single)
    reads = nt((led * read).astype(BF16), single)
    crossing = jnp.sum(state * dstate, axis=0, keepdims=True)
    held = lax.dot_general(
        jnp.broadcast_to(crossing, (8, cols)),
        single.astype(F32),
        (((1,), (1,)), ((), ())),
        precision=HIGH,
        preferred_element_type=F32,
    )[0:1, :]
    held = held * jnp.sum(kd[0, 0:8, :] * pick, axis=0, keepdims=True)
    lower = (s > t).astype(F32)
    upper = (s <= t).astype(F32)
    dlog = (
        jnp.dot(upper, rsum[...].T - csums + reads, precision=HIGH, preferred_element_type=F32)
        + jnp.dot(lower, steps * from_far, precision=HIGH, preferred_element_type=F32)
        + held
    )
    rate = -jnp.exp(alog[0])
    dstep = from_near + from_far + dlog * rate
    ddt = dstep * sigmoid(dtin[0]) * (lane < ha).astype(F32)
    ddt_o[0] = ddt
    hsum_o[0, 0:1, :] += jnp.sum(ddt, axis=0, keepdims=True)
    hsum_o[0, 1:2, :] += jnp.sum(dlog * steps * rate, axis=0, keepdims=True)

    dxs = (near + dx_far) * steps_wide + dyf * skip[...]
    window = pre[pl.ds(pl.multiple_of(c * SPAN, SPAN), SPAN + HALO), :]
    pos = start + iota((SPAN, 1), 0)
    masks = [same_as_behind(sc, pos, j) for j in range(4)]
    lagged = [window[HALO:, :]]
    for j in range(1, 4):
        lagged.append(pltpu.roll(window, j, axis=0)[HALO:, :] * masks[j])
    conv = bias[...]
    for j in range(4):
        conv = conv + taps[j : j + 1, :] * lagged[j]
    sig = sigmoid(conv)
    dconv = dxs * (sig * (1.0 + conv * (1.0 - sig)))
    sums = [jnp.sum(dconv * lagged[j], axis=0, keepdims=True) for j in range(4)]
    sums.append(jnp.sum(dconv, axis=0, keepdims=True))
    csum_o[...] += jnp.concatenate(sums + [jnp.zeros((3, cols), F32)], axis=0)
    dpre = taps[0:1, :] * dconv
    place = iota((SPAN + 8, 1), 0)
    edge = jnp.zeros((HALO, cols), F32)
    blank = jnp.zeros((8, cols), F32)
    for j in range(1, 4):
        masked = dconv * masks[j]
        longer = jnp.concatenate([masked, ahead[8 * (j - 1) : 8 * j, :]], axis=0)
        dpre = dpre + taps[j : j + 1, :] * pltpu.roll(longer, SPAN + 8 - j, axis=0)[:SPAN, :]
        first = masked[:8, :]
        ahead[8 * (j - 1) : 8 * j, :] = first
        before = pltpu.roll(jnp.concatenate([blank, blank, first], axis=0), 24 - j, axis=0)[:HALO, :]
        edge = edge + taps[j : j + 1, :] * before
    dx_o[pl.ds(pl.multiple_of(HALO + c * SPAN, HALO), SPAN), :] = dpre.astype(BF16)

    @pl.when(c == 0)
    def _():
        dx_o[:HALO, :] = edge.astype(BF16)


def run_pull(sc, xs, dy, bc, dtin, dt, lc, lr, em, et, kd, st, sin, ds, dsin, pre, taps, bias, skip, alog, ha, ig):
    count, inner = xs.shape
    total = count + HALO
    chunks = count // SPAN

    def rev(step):
        return chunks - 1 - step

    tile = pl.BlockSpec((SPAN, ig), lambda b, i: (rev(i), b))
    per_block = pl.BlockSpec((1, SPAN, LANES), lambda b, i: (b, rev(i), 0))
    states = pl.BlockSpec((1, LANES, ig), lambda b, i: (rev(i), 0, b))
    edge = pl.BlockSpec((LANES, ig), lambda b, i: (0, b))
    row = pl.BlockSpec((1, ig), lambda b, i: (0, b))
    full = pl.BlockSpec((total, ig), lambda b, i: (0, b))
    return pl.pallas_call(
        partial(pull_body, ha),
        grid=(2, chunks),
        out_shape=(
            jax.ShapeDtypeStruct((total, inner), BF16),
            jax.ShapeDtypeStruct((count, 2 * LANES), F32),
            jax.ShapeDtypeStruct((2, count, LANES), F32),
            jax.ShapeDtypeStruct((8, inner), F32),
            jax.ShapeDtypeStruct((2, 8, LANES), F32),
        ),
        in_specs=[
            scalars(),
            tile,
            tile,
            pl.BlockSpec((SPAN, 2 * LANES), lambda b, i: (rev(i), 0)),
            per_block,
            per_block,
            per_block,
            pl.BlockSpec((1, 16, SPAN), lambda b, i: (b, 0, rev(i))),
            per_block,
            per_block,
            pl.BlockSpec((1, 24, LANES), lambda b, i: (b, 0, 0)),
            states,
            edge,
            states,
            edge,
            full,
            pl.BlockSpec((4, ig), lambda b, i: (0, b)),
            row,
            row,
            pl.BlockSpec((1, 1, LANES), lambda b, i: (b, 0, 0)),
        ],
        out_specs=(
            full,
            pl.BlockSpec((count, 2 * LANES), lambda b, i: (0, 0)),
            per_block,
            pl.BlockSpec((8, ig), lambda b, i: (0, b)),
            pl.BlockSpec((1, 8, LANES), lambda b, i: (b, 0, 0)),
        ),
        scratch_shapes=[
            pltpu.VMEM((SPAN, SPAN), F32),
            pltpu.VMEM((SPAN, SPAN), F32),
            pltpu.VMEM((SPAN, SPAN), F32),
            pltpu.VMEM((24, ig), F32),
            pltpu.VMEM((SPAN, ig), F32),
            pltpu.VMEM((LANES, SPAN), F32),
        ],
        compiler_params=params(),
        cost_estimate=cost(16e9, 30e6),
        name="pull",
    )(sc, xs, dy, bc, dtin, dt, lc, lr, em, et, kd, st, sin, ds, dsin, pre, taps, bias, skip, alog)


def small_body(ha, sc, own, oth, pre, taps, bias, ddt, out, sums_o, scr):
    count = own.shape[0]
    total = count + HALO
    lane = iota((1, LANES), 1)
    steps = ddt[0] + pltpu.roll(ddt[1], ha, axis=1)
    out[:HALO, :] = jnp.zeros((HALO, 3 * LANES), BF16)
    out[HALO:, :LANES] = steps.astype(BF16)
    upstream = own[...].astype(F32) + oth[...].astype(F32)
    pos = sc[3] + iota((count, 1), 0)
    masks = [same_as_behind(sc, pos, j) for j in range(4)]
    lagged = [pre[HALO - j : HALO - j + count, :] * masks[j] for j in range(4)]
    lagged[0] = pre[HALO:, :]
    conv = bias[...]
    for j in range(4):
        conv = conv + taps[j : j + 1, :] * lagged[j]
    sig = sigmoid(conv)
    dconv = upstream * (sig * (1.0 + conv * (1.0 - sig)))
    sums = [jnp.sum(dconv * lagged[j], axis=0, keepdims=True) for j in range(4)]
    sums.append(jnp.sum(dconv, axis=0, keepdims=True))
    sums_o[...] = jnp.concatenate(sums + [jnp.zeros((3, 2 * LANES), F32)], axis=0)
    scr[...] = jnp.zeros_like(scr)
    dpre = jnp.zeros((total, 2 * LANES), F32)
    for j in range(4):
        scr[HALO : HALO + count, :] = dconv * masks[j] if j else dconv
        dpre = dpre + taps[j : j + 1, :] * scr[j : j + total, :]
    out[:, LANES:] = dpre.astype(BF16)


def run_small(sc, own, oth, pre, taps, bias, ddt, ha):
    count = own.shape[0]
    total = count + HALO
    return pl.pallas_call(
        partial(small_body, ha),
        out_shape=(
            jax.ShapeDtypeStruct((total, 3 * LANES), BF16),
            jax.ShapeDtypeStruct((8, 2 * LANES), F32),
        ),
        in_specs=[scalars()] + [whole()] * 6,
        out_specs=[whole()] * 2,
        scratch_shapes=[pltpu.VMEM((total + 8, 2 * LANES), F32)],
        compiler_params=params(),
        cost_estimate=cost(1e8, 4e6),
        name="small",
    )(sc, own, oth, pre, taps, bias, ddt)


def dnorm_body(lists, rows, share, sc, dz, dx, dsmall, tok, *rest):
    counts = [len(parts) for parts in lists]
    total_refs = sum(counts)
    refs = rest[:total_refs]
    out, sums, scr_z, scr_x, scr_s = rest[total_refs:]
    cols = out.shape[1]
    j = pl.program_id(0)

    @pl.when(j == 0)
    def _():
        low = 0
        for parts, scr in zip(lists, (scr_z, scr_x, scr_s)):
            assemble(sc[4], rows, parts, refs[low : low + len(parts)], scr)
            low += len(parts)

    at = pl.ds(pl.multiple_of(j * cols, cols), cols)
    w_s = scr_s[at, :]
    value = (
        nt(dx[...], scr_x[at, :])
        + nt(dsmall[:, :LANES], w_s[:, :LANES])
        + nt(dsmall[:, LANES:], w_s[:, LANES:]) * share
    )
    from_z = nt(dz[...], scr_z[at, :])
    top = value[:HALO, :]
    rest_v = value[HALO:, :] + from_z
    out[:HALO, :] = top.astype(BF16)
    out[HALO:, :] = rest_v.astype(BF16)
    total = jnp.sum(top * tok[:HALO, :].astype(F32), axis=0, keepdims=True) + jnp.sum(
        rest_v * tok[HALO:, :].astype(F32), axis=0, keepdims=True
    )
    sums[...] = jnp.broadcast_to(total, sums.shape)


def run_dnorm(sc, dz, dx, dsmall, tok, pieces_z, pieces_x, pieces_s, rows, share):
    total, width = tok.shape
    inner = dx.shape[1]
    cols = 256
    lists = [pieces_z[0], pieces_x[0], pieces_s[0]]
    refs = [*pieces_z[1], *pieces_x[1], *pieces_s[1]]
    return pl.pallas_call(
        partial(dnorm_body, lists, rows, share),
        grid=(width // cols,),
        out_shape=(
            jax.ShapeDtypeStruct((total, width), BF16),
            jax.ShapeDtypeStruct((8, width), F32),
        ),
        in_specs=[scalars(), whole(), whole(), whole(), pl.BlockSpec((total, cols), lambda j: (0, j))]
        + [whole()] * len(refs),
        out_specs=(
            pl.BlockSpec((total, cols), lambda j: (0, j)),
            pl.BlockSpec((8, cols), lambda j: (0, j)),
        ),
        scratch_shapes=[
            pltpu.VMEM((width, inner), BF16),
            pltpu.VMEM((width, inner), BF16),
            pltpu.VMEM((width, 3 * LANES), BF16),
        ],
        compiler_params=params(),
        cost_estimate=cost(2 * total * width * (2 * inner + 384), 20e6),
        name="dnorm",
    )(sc, dz, dx, dsmall, tok, *refs)


def swap(value, bit, size):
    return lax.ppermute(value, "dp", [(i, i ^ bit) for i in range(size)])


def link_bits(size):
    bits = []
    bit = 2
    while bit < size:
        bits.append(bit)
        bit *= 2
    return bits


def gather_rows(shard, split, size):
    parts, refs = [], []
    bits = link_bits(size)
    for low, high, order in ((0, split, bits), (split, shard.shape[1], bits[::-1])):
        held, names = shard[None, :, low:high], [0]
        stacks = []
        for position, bit in enumerate(order):
            got = swap(held, bit, size)
            new = [v ^ bit for v in names]
            if position + 1 < len(order):
                held, names = jnp.concatenate([held, got], axis=0), names + new
            else:
                stacks = [(held, names), (got, new)]
        for stack, named in stacks:
            parts.append((tuple(named), low))
            refs.append(stack)
        for stack, named in stacks:
            parts.append((tuple(v ^ 1 for v in named), low))
            refs.append(swap(stack, 1, size))
    return parts, refs


def scatter_rows(own, oth, split, size):
    got = swap(oth, 1, size)
    outs = []
    bits = link_bits(size)
    for low, high, order in ((0, split, bits), (split, own.shape[2], bits[::-1])):
        held = {2 * u: own[u, :, low:high].astype(F32) + got[u, :, low:high].astype(F32) for u in range(own.shape[0])}
        for bit in order:
            away = sorted(v for v in held if v & bit)
            stay = sorted(v for v in held if not v & bit)
            arrived = swap(jnp.stack([held[v].astype(BF16) for v in away]), bit, size)
            held = {v: held[v] + arrived[i].astype(F32) for i, v in enumerate(stay)}
        outs.append(held[0].astype(BF16))
    return outs


def to_heads(shard, parts, lower):
    hp = parts // 2
    first = [(2 * p, p) for p in range(hp)] + [(2 * (p - hp) + 1, p) for p in range(hp, parts)]
    second = [(2 * p + 1, p) for p in range(hp)] + [(2 * (p - hp), p) for p in range(hp, parts)]
    one, two = lax.ppermute(shard, "tensor", first), lax.ppermute(shard, "tensor", second)
    return jnp.where(lower, one, two), jnp.where(lower, two, one)


def from_heads(block_a, block_b, parts, lower):
    hp = parts // 2
    first = [(p, 2 * p) for p in range(hp)] + [(p, 2 * (p - hp) + 1) for p in range(hp, parts)]
    second = [(p, 2 * p + 1) for p in range(hp)] + [(p, 2 * (p - hp)) for p in range(hp, parts)]
    one = lax.ppermute(jnp.where(lower, block_a, block_b), "tensor", first)
    two = lax.ppermute(jnp.where(lower, block_b, block_a), "tensor", second)
    return one.astype(F32) + two.astype(F32)


def half_groups(parts):
    hp = parts // 2
    return [list(range(hp)), list(range(hp, parts))]


def half_gather(value, parts, place):
    hp = parts // 2
    if hp != 2:
        return lax.all_gather(value, "tensor", axis=0, tiled=True, axis_index_groups=half_groups(parts))
    other = lax.ppermute(value, "tensor", [(p, p ^ 1) for p in range(parts)])
    return jnp.where(
        place == 0, jnp.concatenate([value, other], axis=0), jnp.concatenate([other, value], axis=0)
    )


def half_other(value, parts):
    hp = parts // 2
    total = jnp.zeros(value.shape, F32)
    for shift in range(1, hp):
        pairs = [(p, (p // hp) * hp + (p % hp + shift) % hp) for p in range(parts)]
        total = total + lax.ppermute(value, "tensor", pairs).astype(F32)
    return total if hp > 2 else lax.ppermute(value, "tensor", [(p, p ^ 1) for p in range(parts)])


def half_scatter(value, parts, place):
    hp = parts // 2
    rows = value.shape[0] // hp
    mine = lax.dynamic_slice_in_dim(value, place * rows, rows, 0)
    total = mine.astype(F32)
    for shift in range(1, hp):
        pairs = [(p, (p // hp) * hp + (p % hp + shift) % hp) for p in range(parts)]
        away = lax.dynamic_slice_in_dim(value, lax.rem(place + shift, hp) * rows, rows, 0)
        total = total + lax.ppermute(away, "tensor", pairs).astype(F32)
    return total


def sum_dp(value, size):
    bit = 1
    while bit < size:
        value = value + swap(value, bit, size)
        bit *= 2
    return value


def sum_tensor(value, parts):
    bit = 1
    while bit < parts:
        value = value + lax.ppermute(value, "tensor", [(p, p ^ bit) for p in range(parts)])
        bit *= 2
    return value


def after(value, *others):
    return lax.optimization_barrier((value, *others))[0]


def local(
    inputs,
    cotangent,
    seq_lengths,
    norm_gain,
    w_z,
    w_x,
    w_bc,
    w_dt,
    conv_x,
    conv_x_bias,
    conv_bc,
    conv_bc_bias,
    dt_bias,
    a_log,
    d_skip,
    gate_gain,
    w_out,
):
    local_rows, width = inputs.shape
    parts = lax.axis_size("tensor")
    size = lax.axis_size("dp")
    hp = parts // 2
    position = lax.axis_index("tensor")
    me = lax.axis_index("dp")
    lower = position < hp
    place = lax.rem(position, hp)
    count = local_rows * hp
    ha = dt_bias.shape[0]
    ig = w_z.shape[1]
    inner = 2 * ig
    inner_all = ig * parts
    rows = w_z.shape[0]
    head_width = ig // ha

    ends = [seq_lengths[0, 0], seq_lengths[0, 0] + seq_lengths[0, 1]]
    ends.append(ends[1] + seq_lengths[0, 2])
    base = jnp.where(lower, 0, count)
    sc = jnp.stack([*ends, base, me, position, position, position]).astype(jnp.int32)

    def pad(v, to):
        return jnp.pad(v, [(0, 0)] * (v.ndim - 1) + [(0, to - v.shape[-1])])

    heads_row = jnp.concatenate([pad(dt_bias, LANES), pad(a_log, LANES), pad(d_skip, LANES)])
    table = jnp.concatenate(
        [conv_x, conv_x_bias[None], gate_gain[None], jnp.repeat(d_skip, head_width)[None], pad(heads_row, ig)[None]]
    )
    par_a, par_b = to_heads(table, parts, lower)
    wide = jnp.concatenate([par_a, par_b], axis=1)
    taps_x, bias_x, gain, skip = wide[0:4], wide[4:5], wide[5:6], wide[6:7]
    dtb = jnp.concatenate([par_a[7, :ha], par_b[7, :ha], jnp.zeros((LANES - 2 * ha,), F32)])[None]
    alog = jnp.concatenate([par_a[7, LANES : LANES + ha], par_b[7, LANES : LANES + ha], jnp.zeros((LANES - 2 * ha,), F32)])[None]
    alog_blocks = jnp.stack([par_a[7, LANES : 2 * LANES], par_b[7, LANES : 2 * LANES]])[:, None, :]

    dt_a, dt_b = to_heads(w_dt, parts, lower)
    small = jnp.concatenate([dt_a, dt_b, jnp.zeros((rows, LANES - 2 * ha), BF16), w_bc], axis=1)
    p_small = gather_rows(small, LANES, size)
    x_a, x_b = to_heads(w_x, parts, lower)
    p_x = gather_rows(jnp.concatenate([x_a, x_b], axis=1), ig, size)
    z_a, z_b = to_heads(after(w_z, x_a), parts, lower)
    p_z = gather_rows(jnp.concatenate([z_a, z_b], axis=1), ig, size)
    o_a, o_b = to_heads(after(w_out, z_a).T, parts, lower)
    p_o = gather_rows(jnp.concatenate([o_a, o_b], axis=1), ig, size)

    input_f = inputs.astype(F32)
    in_scale = lax.rsqrt(jnp.mean(input_f * input_f, axis=1, keepdims=True) + EPS)
    normed = (input_f * in_scale * norm_gain[None, :]).astype(BF16)
    halo = jnp.zeros((HALO, width), BF16)
    for k in range(hp):
        halo = halo + lax.ppermute(normed[local_rows - HALO :], "tensor", [(hp - 1, hp + k)])
    tok = jnp.concatenate([halo, half_gather(normed, parts, place)], axis=0)
    pulled = half_gather(after(cotangent, tok), parts, place)

    pre_bc, bc, dtin, dt, lc, lr, em, et, kd = run_maps(
        sc, tok, conv_bc, conv_bc_bias[None], dtb, alog, p_small, rows, ha
    )
    pre_x, xs, st, fin = run_xpath(sc, tok, taps_x, bias_x, bc, dt, et, kd, p_x, rows, ig)
    forward = [(p, p + hp) for p in range(hp)]
    sin = lax.ppermute(fin, "tensor", forward)
    z = run_proj(sc, tok, p_z, rows, inner, count)
    dm = run_proj(sc, pulled, p_o, rows, inner, count)
    y, stat = run_scan(sc, xs, bc, dt, lc, lr, em, kd, st, sin, z, dm, skip, gain, ig)
    stat_other = half_other(stat, parts)
    mixed, dz, dy, gate_sums, ds, dfirst = run_gate(
        sc, y, z, dm, stat, stat_other, xs, gain, bc, em, kd, ig, inner_all
    )
    dsin = lax.ppermute(dfirst, "tensor", [(p + hp, p) for p in range(hp)])
    branch = run_back(sc, mixed, p_o, rows, width)
    outputs = (input_f + half_scatter(branch, parts, place)).astype(BF16)
    gw_o = run_grad(sc, pulled, mixed, rows)
    gw_z = run_grad(sc, tok, dz, rows)
    dx, dbc, ddt, conv_sums, head_sums = run_pull(
        sc, xs, dy, bc, dtin, dt, lc, lr, em, et, kd, st, sin, ds, dsin, pre_x, taps_x, bias_x, skip,
        alog_blocks, ha, ig,
    )
    dbc_low = dbc.astype(BF16)
    dbc_other = half_other(dbc_low, parts)
    gw_x = run_grad(sc, tok, dx, rows)
    dsmall, bc_sums = run_small(sc, dbc_low, dbc_other, pre_bc, conv_bc, conv_bc_bias[None], ddt, ha)
    dn, norm_sums = run_dnorm(sc, dz, dx, dsmall, tok, p_z, p_x, p_small, rows, 1.0 / hp)
    gw_s = run_grad(sc, tok, dsmall, rows)

    dn_own = half_scatter(dn[HALO:], parts, place)
    edge = jnp.zeros((HALO, width), F32)
    for k in range(hp):
        edge = edge + lax.ppermute(dn[:HALO], "tensor", [(hp + k, hp - 1)]).astype(F32)
    dn_own = dn_own + jnp.concatenate([jnp.zeros((local_rows - HALO, width), F32), edge], axis=0)
    dnorm_side = dn_own * norm_gain[None, :]
    grad_inputs = (
        in_scale * dnorm_side
        - input_f
        * (in_scale * in_scale * in_scale)
        * (jnp.sum(dnorm_side * input_f, axis=1, keepdims=True) / width)
        + cotangent.astype(F32)
    ).astype(BF16)

    grad_w_out = from_heads(*scatter_rows(*gw_o, ig, size), parts, lower).T
    grad_w_z = from_heads(*scatter_rows(*gw_z, ig, size), parts, lower)
    grad_w_x = from_heads(*scatter_rows(*gw_x, ig, size), parts, lower)
    s_dt, s_bc = scatter_rows(*gw_s, LANES, size)
    grad_w_dt = from_heads(s_dt[:, :ha], s_dt[:, ha : 2 * ha], parts, lower)
    grad_w_bc = s_bc.astype(F32) + lax.ppermute(
        s_bc, "tensor", [(p, (p + hp) % parts) for p in range(parts)]
    ).astype(F32)

    heads_row = pad(head_sums[:, :2].reshape(2, 2 * LANES), ig).reshape(1, inner)
    chan = jnp.concatenate([conv_sums[:5], gate_sums[:2], heads_row])
    rep = jnp.concatenate([(norm_sums[0] / norm_gain), bc_sums[:5].reshape(-1) / hp])
    chan = sum_dp(chan, size)
    chan = from_heads(chan[:, :ig], chan[:, ig:], parts, lower)
    rep = sum_tensor(sum_dp(rep.reshape(-1, LANES), size), parts).reshape(-1)
    rep_bc = rep[width:].reshape(5, -1)
    return (
        outputs,
        grad_inputs,
        rep[:width],
        grad_w_z,
        grad_w_x,
        grad_w_bc,
        grad_w_dt,
        chan[:4],
        chan[4],
        rep_bc[:4],
        rep_bc[4],
        chan[7, :ha],
        chan[7, LANES : LANES + ha],
        jnp.sum(chan[6].reshape(ha, head_width), axis=1),
        chan[5],
        grad_w_out,
    )


def solution(mesh):
    tokens = P(("dp", "tensor"), None)
    matrix = P("dp", "tensor")
    heads = P("tensor")
    return jax.shard_map(
        local,
        mesh=mesh,
        in_specs=(
            tokens,
            tokens,
            P("dp", None),
            P(),
            matrix,
            matrix,
            P("dp", None),
            matrix,
            P(None, "tensor"),
            heads,
            P(),
            P(),
            heads,
            heads,
            heads,
            heads,
            P("tensor", "dp"),
        ),
        out_specs=(
            tokens,
            tokens,
            P(),
            matrix,
            matrix,
            P("dp", None),
            matrix,
            P(None, "tensor"),
            heads,
            P(),
            P(),
            heads,
            heads,
            heads,
            heads,
            P("tensor", "dp"),
        ),
        check_vma=False,
    )
```

time: 1280 us -> 549 us (0.43)
  waiting for transfers between devices: 537 us -> 167 us
  matrix products: 318 us -> 0 us
  Pallas kernels: 0 us -> 183 us
  other arithmetic: 190 us -> 52.5 us
  local copies, waits for them, and re-layouts: 159 us -> 26.3 us
  starting transfers between devices: 0.74 us -> 111 us
  blocking collectives: 40.5 us -> 0 us
    dot_general x87 -> x0, matrix products: 318 us -> none  [the longest x18 118 us: block_step(): local_part = jnp.einsum('tsh,shp->thp', mixing, x_block, precision=highest)]
    reduce_scatter x6 -> x0, waiting for transfers between devices: 273 us -> none  [the longest x1 85.7 us: local(): lax.psum_scatter(contribution.astype(jnp.bfloat16), 'tensor', scatter_dim...]
    pallas_call x0 -> x14, Pallas kernels: none -> 183 us  [the longest x1 40.8 us: run_pull(): pl.pallas_call(partial(pull_body, ha), grid=(2, chunks), out_shape=(jax.S...]
    psum x2 -> x0, waiting for transfers between devices: 169 us -> none  [the longest x1 132 us: local(): lax.psum((grad_norm_gain, widen(grad_conv_x, parts, position, 1), widen(g...]
    ppermute x0 -> x93, waiting for transfers between devices: none -> 167 us  [the longest x58 75.7 us: swap(): return lax.ppermute(value, 'dp', [(i, i ^ bit) for i in range(size)])]
    ppermute x0 -> x93, starting transfers between devices: none -> 111 us  [the longest x58 43.2 us: swap(): return lax.ppermute(value, 'dp', [(i, i ^ bit) for i in range(size)])]
    all_gather x5 -> x0, waiting for transfers between devices: 92.4 us -> none  [the longest x1 64.6 us: local(): lax.all_gather(normed, 'tensor', axis=0, tiled=True)]
    dynamic_update_slice x44 -> x0, other arithmetic: 61 us -> none  [the longest x42 60.7 us: run_scan(): _, ys = lax.scan(partial(block_step, rate), begin, pieces)]
  transfers between devices with their start and end apart: 14 -> 93, of which waited for: 9 -> 35; matrix products, arithmetic and copies ran while one was open for 29% -> 12% of each run, Pallas kernels for 0% -> 21%
where the time goes in v1:
time: 549 us; the launch traced here: 544 us
  Pallas kernels  183 us (33%)
  waiting for transfers between devices  167 us (30%)
  starting transfers between devices  111 us (20%)
  other arithmetic  52.5 us (10%)
  local copies, waits for them, and re-layouts  26.3 us (5%)
    ppermute x58, waiting for transfers between devices, swap(): return lax.ppermute(value, 'dp', [(i, i ^ bit) for i in range(size)])  75.7 us
    ppermute x58, starting transfers between devices, swap(): return lax.ppermute(value, 'dp', [(i, i ^ bit) for i in range(size)])  43.2 us
    pallas_call x1, Pallas kernels, run_pull(): pl.pallas_call(partial(pull_body, ha), grid=(2, chunks), out_shape=(jax.S...  40.8 us
    pallas_call x4, Pallas kernels, run_grad(): pl.pallas_call(partial(grad_body, rows), grid=(inner // cols,), out_shape...  33.3 us
    ppermute x2, waiting for transfers between devices, sum_tensor(): lax.ppermute(value, 'tensor', [(p, p ^ bit) for p in range(parts)])  26.1 us
    pallas_call x1, Pallas kernels, run_xpath(): pl.pallas_call(partial(xpath_body, parts, rows, ig), grid=(inner // cols,...  20.1 us
    pallas_call x2, Pallas kernels, run_proj(): pl.pallas_call(partial(proj_body, parts, rows), grid=(inner // cols,), ou...  18.8 us
    pallas_call x1, Pallas kernels, run_dnorm(): pl.pallas_call(partial(dnorm_body, lists, rows, share), grid=(width // co...  18 us
  transfers between devices with their start and end apart: 93, of which 35 were waited for; matrix products, arithmetic and copies ran while one was open for 12% of the time, Pallas kernels for 21%

profile of v1, /device:TPU:8, one launch (start us, length us, event | category | flops | bytes accessed | tf_op | source)
XLA Modules:
  0.0 544.1 jit_solution(14266328220866609587)
XLA Ops:
  5.0 5.0 collective-permute-start.3
  10.9 2.3 collective-permute-start.5
  15.9 3.4 collective-permute-start.15
  19.3 4.0 collective-permute-done.5
  25.5 3.7 collective-permute-done.15
  29.3 3.0 collective-permute-start.26
  32.8 3.4 collective-permute-start.1
  40.6 4.7 collective-permute-done.26
  49.4 3.6 collective-permute-start.37
  74.3 3.6 collective-permute-done.28
  79.5 4.8 collective-permute-done.39
  86.4 9.7 %collective-permute-done.22.rest_5_.rest_13_ = bf16[2,192,768]{2,1,0:T(8,128)(2,1)S(1)} collective-permute-done((bf16[2,192,768]{2,1,0:T(8,128)(2,1)S(1)}, bf16[2,192,768]{2,1,0:T(8,128)(2,1)S(1)}, u32[]{:S(2)}, u32[]{:S(2)}) %collective-permute-start.22) | collective-permute-done | bytes 589856 | tf_op jit(solution)/shard_map/ppermute | solution.py:837
  103.2 7.6 %collective-permute-done.33.rest_5_ = bf16[2,192,768]{2,1,0:T(8,128)(2,1)} collective-permute-done((bf16[2,192,768]{2,1,0:T(8,128)(2,1)S(1)}, bf16[2,192,768]{2,1,0:T(8,128)(2,1)}, u32[]{:S(2)}, u32[]{:S(2)}) %collective-permute-start.33) | collective-permute-done | bytes 589856 | tf_op jit(solution)/shard_map/ppermute | solution.py:837
  110.8 2.1 collective-permute-start.36
  118.0 7.8 %maps.1 = (f32[784,256]{1,0:T(8,128)}, bf16[768,256]{1,0:T(8,128)(2,1)}, f32[2,768,128]{2,1,0:T(8,128)}, f32[2,768,128]{2,1,0:T(8,128)}, f32[2,768,128]{2,1,0:T(...) custom-call(s32[8]{0:T(128)} %stack.35.sc, ...), custom_call_target="tpu_custom_call" | custom-call | flops 1233125376 | bytes 8000000 | tf_op jit(solution)/shard_map/maps/pallas_call | solution.py:159
  125.7 20.1 %xpath.1 = (f32[784,1536]{1,0:T(8,128)}, bf16[768,1536]{1,0:T(8,128)(2,1)}, f32[3,128,1536]{2,1,0:T(8,128)}, bf16[128,1536]{1,0:T(8,128)(2,1)}) custom-call(s32[8]{0:T(128)} %stack.35.sc, bf16[784,1536]{1,0:T(8,128)(2,1)} %pad_maximum_fusion.tok.x, f32[4,1536]{1,0:T(4,128)} %fusion.11.taps, f32[1,1536]{1,0:T(1,128)} %get-tuple-element.163.bias, ...), custom_call_target="tpu_custom_call" | custom-call | flops 4439251456 | bytes 20000000 | tf_op jit(solution)/shard_map/xpath/pallas_call | solution.py:223
  147.2 9.4 %proj.2.z = f32[768,1536]{1,0:T(8,128)} custom-call(s32[8]{0:T(128)} %stack.35.sc, bf16[784,1536]{1,0:T(8,128)(2,1)} %pad_maximum_fusion.tok.x, bf16[2,192,768]{2,1,0:T(8,128)(2,1)} %copy-done.13, bf16[2,192,768]{2,1,0:T(8,128)(2,1)} %collective-permute-done.29.rest_1_, bf16[2,192,768]{2,1,0:T(8,128)(2,1)} %copy-done.43, ...), custom_call_target="tpu_custom_call" | custom-call | flops 3623878656 | bytes 12000000 | tf_op jit(solution)/shard_map/proj/pallas_call | solution.py:274
  156.6 4.0 collective-permute-start.25
  160.6 1.8 maximum_select_fusion.1.x
  162.4 9.4 %proj.3.dm = f32[768,1536]{1,0:T(8,128)} custom-call(s32[8]{0:T(128)} %stack.35.sc, bf16[768,1536]{1,0:T(8,128)(2,1)} %maximum_select_fusion.1.x, bf16[2,192,768]{2,1,0:T(8,128)(2,1)} %pad_maximum_fusion.5.rest_0_, bf16[2,192,768]{2,1,0:T(8,128)(2,1)} %collective-permute-done.40.rest_1_, bf16[2,192,768]{2,1,0:T(8,128)(2,1)} %collective-permute-done.41.rest_2_, ...), custom_call_target="tpu_custom_call" | custom-call | flops 3623878656 | bytes 12000000 | tf_op jit(solution)/shard_map/proj/pallas_call | solution.py:274
  171.8 5.8 %collective-permute-done.25.sin = bf16[128,1536]{1,0:T(8,128)(2,1)S(1)} collective-permute-done((bf16[128,1536]{1,0:T(8,128)(2,1)}, bf16[128,1536]{1,0:T(8,128)(2,1)S(1)}, u32[]{:S(2)}, u32[]{:S(2)}) %collective-permute-start.25) | collective-permute-done | bytes 393248 | tf_op jit(solution)/shard_map/ppermute | solution.py:1037
  178.4 14.6 %scan.1 = (f32[768,1536]{1,0:T(8,128)}, f32[768,128]{1,0:T(8,128)}) custom-call(s32[8]{0:T(128)} %stack.35.sc, bf16[768,1536]{1,0:T(8,128)(2,1)} %get-tuple-element.61.xs, bf16[768,256]{1,0:T(8,128)(2,1)} %get-tuple-element.57.bc, f32[2,768,128]{2,1,0:T(8,128)} %get-tuple-element.58.dt, f32[2,768,128]{2,1,0:T(8,128)} %get-tuple-element.62.lc, ...), custom_call_target="tpu_custom_call" | custom-call | flops 6000000000 | bytes 20000000 | tf_op jit(solution)/shard_map/scan/pallas_call | solution.py:402
  194.5 9.2 %collective-permute-done.47.stat_b = f32[768,128]{1,0:T(8,128)S(1)} collective-permute-done((f32[768,128]{1,0:T(8,128)}, f32[768,128]{1,0:T(8,128)S(1)}, u32[]{:S(2)}, u32[]{:S(2)}) %collective-permute-start.47) | collective-permute-done | bytes 393248 | tf_op jit(solution)/shard_map/ppermute | solution.py:924
  204.5 13.7 %gate.1 = (bf16[768,1536]{1,0:T(8,128)(2,1)}, bf16[768,1536]{1,0:T(8,128)(2,1)}, bf16[768,1536]{1,0:T(8,128)(2,1)}, f32[8,1536]{1,0:T(8,128)}, f32[3,128,1536]{2,1,0:T(8,128)}, /*index=5*/bf16[128,1536]{1,0:T(8,128)(2,1)}) custom-call(s32[8]{0:T(128)} %stack.35.sc, f32[768,1536]{1,0:T(8,128)} %get-tuple-element.70.y, f32[768,1536]{1,0:T(8,128)} %proj.2.z, ...), custom_call_target="tpu_custom_call" | custom-call | flops 4000000000 | bytes 30000000 | tf_op jit(solution)/shard_map/gate/pallas_call | solution.py:473
  220.8 8.9 %grad.7 = (bf16[4,192,1536]{2,1,0:T(8,128)(2,1)}, bf16[4,192,1536]{2,1,0:T(8,128)(2,1)}) custom-call(s32[8]{0:T(128)} %stack.35.sc, bf16[768,1536]{1,0:T(8,128)(2,1)} %maximum_select_fusion.1.x, bf16[768,1536]{1,0:T(8,128)(2,1)} %get-tuple-element.72.x.y), custom_call_target="tpu_custom_call" | custom-call | flops 3623878656 | bytes 10000000 | tf_op jit(solution)/shard_map/grad/pallas_call | solution.py:336
  231.5 40.8 %pull.1 = (bf16[784,1536]{1,0:T(8,128)(2,1)}, f32[768,256]{1,0:T(8,128)}, f32[2,768,128]{2,1,0:T(8,128)}, f32[8,1536]{1,0:T(8,128)}, f32[2,8,128]{2,1,0:T(8,128)}) custom-call(s32[8]{0:T(128)} %stack.35.sc, bf16[768,1536]{1,0:T(8,128)(2,1)} %get-tuple-element.61.xs, bf16[768,1536]{1,0:T(8,128)(2,1)} %get-tuple-element.74.dy, ...), custom_call_target="tpu_custom_call" | custom-call | flops 16000000000 | bytes 30000000 | tf_op jit(solution)/shard_map/pull/pallas_call | solution.py:674
  273.9 9.3 %back.1 = bf16[768,1536]{1,0:T(8,128)(2,1)} custom-call(s32[8]{0:T(128)} %stack.35.sc, bf16[768,1536]{1,0:T(8,128)(2,1)} %get-tuple-element.72.x.y, bf16[2,192,768]{2,1,0:T(8,128)(2,1)} %pad_maximum_fusion.5.rest_0_, bf16[2,192,768]{2,1,0:T(8,128)(2,1)} %collective-permute-done.40.rest_1_, bf16[2,192,768]{2,1,0:T(8,128)(2,1)} %collective-permute-done.41.rest_2_, ...), custom_call_target="tpu_custom_call" | custom-call | flops 3623878656 | bytes 10000000 | tf_op jit(solution)/shard_map/back/pallas_call | solution.py:304
  283.8 2.4 constant_dynamic-slice_fusion.1
  286.2 8.9 %collective-permute-start.48 = (bf16[384,1536]{1,0:T(8,128)(2,1)}, bf16[384,1536]{1,0:T(8,128)(2,1)}, u32[]{:S(2)}, u32[]{:S(2)}) collective-permute-start(bf16[384,1536]{1,0:T(8,128)(2,1)} %constant_dynamic-slice_fusion.1), channel_id=1, source_target_pairs={{0,1},{1,0},{2,3},{3,2},{4,5},{5,4},{6,7},{7,6},{8,9},{9,8},{10,11... | collective-permute-start | bytes 3538952 | tf_op jit(solution)/shard_map/ppermute | solution.py:935
  295.7 9.0 %grad.4 = (bf16[4,192,1536]{2,1,0:T(8,128)(2,1)}, bf16[4,192,1536]{2,1,0:T(8,128)(2,1)}) custom-call(s32[8]{0:T(128)} %stack.35.sc, bf16[784,1536]{1,0:T(8,128)(2,1)} %pad_maximum_fusion.tok.x, bf16[768,1536]{1,0:T(8,128)(2,1)} %get-tuple-element.73.dz.y), custom_call_target="tpu_custom_call" | custom-call | flops 3623878656 | bytes 10000000 | tf_op jit(solution)/shard_map/grad/pallas_call | solution.py:336
  306.1 4.3 collective-permute-start.84
  310.5 9.8 %grad.5 = (bf16[4,192,1536]{2,1,0:T(8,128)(2,1)}, bf16[4,192,1536]{2,1,0:T(8,128)(2,1)}) custom-call(s32[8]{0:T(128)} %stack.35.sc, bf16[784,1536]{1,0:T(8,128)(2,1)} %pad_maximum_fusion.tok.x, bf16[784,1536]{1,0:T(8,128)(2,1)} %get-tuple-element.79.dx.y), custom_call_target="tpu_custom_call" | custom-call | flops 3699376128 | bytes 10000000 | tf_op jit(solution)/shard_map/grad/pallas_call | solution.py:336
  320.3 10.3 %collective-permute-done.85 = f32[8,768]{1,0:T(8,128)S(1)} collective-permute-done((f32[8,768]{1,0:T(8,128)S(1)}, f32[8,768]{1,0:T(8,128)S(1)}, u32[]{:S(2)}, u32[]{:S(2)}) %collective-permute-start.85) | collective-permute-done | bytes 24608 | tf_op jit(solution)/shard_map/ppermute | solution.py:899
  331.4 6.8 %small.1 = (bf16[784,384]{1,0:T(8,128)(2,1)}, f32[8,256]{1,0:T(8,128)}) custom-call(s32[8]{0:T(128)} %stack.35.sc, bf16[768,256]{1,0:T(8,128)(2,1)} %copy-done.7, bf16[768,256]{1,0:T(8,128)(2,1)} %copy-done.15, f32[784,256]{1,0:T(8,128)} %get-tuple-element.81.pre, f32[4,256]{1,0:T(4,128)} %taps.3, f32[1,256]{1,0:T(1,128)} %bitcast.88, ...), custom_call_target="tpu_custom_call" | custom-call | flops 100000000 | bytes 4000000 | tf_op jit(solution)/shard_map/small/pallas_call | solution.py:758
  338.2 18.0 %dnorm.1 = (bf16[784,1536]{1,0:T(8,128)(2,1)}, f32[8,1536]{1,0:T(8,128)}) custom-call(s32[8]{0:T(128)} %stack.35.sc, bf16[768,1536]{1,0:T(8,128)(2,1)} %get-tuple-element.73.dz.y, bf16[784,1536]{1,0:T(8,128)(2,1)} %get-tuple-element.79.dx.y, bf16[784,384]{1,0:T(8,128)(2,1)} %get-tuple-element.83.dsmall.y, bf16[784,1536]{1,0:T(8,128)(2,1)} %pad_maximum_fusion.tok.x, ...), custom_call_target="tpu_custom_call" | custom-call | flops 8323596288 | bytes 20000000 | tf_op jit(solution)/shard_map/dnorm/pallas_call | solution.py:812
  363.2 1.8 slice.370
  369.9 2.1 collective-permute-done.56
  372.5 5.5 %grad.6 = (bf16[4,192,384]{2,1,0:T(8,128)(2,1)}, bf16[4,192,384]{2,1,0:T(8,128)(2,1)}) custom-call(s32[8]{0:T(128)} %stack.35.sc, bf16[784,1536]{1,0:T(8,128)(2,1)} %pad_maximum_fusion.tok.x, bf16[784,384]{1,0:T(8,128)(2,1)} %get-tuple-element.83.dsmall.y), custom_call_target="tpu_custom_call" | custom-call | flops 924844032 | bytes 10000000 | tf_op jit(solution)/shard_map/grad/pallas_call | solution.py:336
  378.2 1.6 collective-permute-start.51
  379.8 2.9 collective-permute-start.58
  383.4 26.1 %collective-permute-done.58 = f32[22,128]{1,0:T(8,128)S(1)} collective-permute-done((f32[22,128]{1,0:T(8,128)S(1)}, f32[22,128]{1,0:T(8,128)S(1)}, u32[]{:S(2)}, u32[]{:S(2)}) %collective-permute-start.58) | collective-permute-done | bytes 11296 | tf_op jit(solution)/shard_map/ppermute | solution.py:950
  412.6 3.1 collective-permute-done.77
  418.7 2.0 collective-permute-done.78
  422.2 1.9 collective-permute-start.79
  424.2 1.6 add_convert_fusion.25
  428.5 2.2 collective-permute-done.75
  431.0 1.7 fusion.9
  432.7 2.6 collective-permute-done.80
  435.3 1.6 collective-permute-start.76
  441.2 1.6 convert_add_fusion.3
  442.8 1.9 fusion.8
  444.9 4.5 fusion.7
  449.4 1.7 add_convert_fusion.19
  453.0 1.7 add_convert_fusion.3
  458.4 9.0 %collective-permute-done.60 = bf16[2,192,768]{2,1,0:T(8,128)(2,1)S(1)} collective-permute-done((bf16[2,192,768]{2,1,0:T(8,128)(2,1)S(1)}, bf16[2,192,768]{2,1,0:T(8,128)(2,1)S(1)}, u32[]{:S(2)}, u32[]{:S(2)}) %collective-permute-start.60) | collective-permute-done | bytes 589856 | tf_op jit(solution)/shard_map/ppermute | solution.py:837
  472.0 7.9 %collective-permute-done.87 = bf16[2,192,768]{2,1,0:T(8,128)(2,1)S(1)} collective-permute-done((bf16[2,192,768]{2,1,0:T(8,128)(2,1)S(1)}, bf16[2,192,768]{2,1,0:T(8,128)(2,1)S(1)}, u32[]{:S(2)}, u32[]{:S(2)}) %collective-permute-start.87) | collective-permute-done | bytes 589856 | tf_op jit(solution)/shard_map/ppermute | solution.py:837
  483.5 15.4 %collective-permute-done.63 = bf16[1,192,768]{2,1,0:T(8,128)(2,1)S(1)} collective-permute-done((bf16[1,192,768]{2,1,0:T(8,128)(2,1)S(1)}, bf16[1,192,768]{2,1,0:T(8,128)(2,1)S(1)}, u32[]{:S(2)}, u32[]{:S(2)}) %collective-permute-start.63) | collective-permute-done | bytes 294944 | tf_op jit(solution)/shard_map/ppermute | solution.py:837
  503.1 4.2 collective-permute-start.64
  510.6 4.4 collective-permute-done.70
  515.1 2.2 collective-permute-start.91
  517.8 3.6 collective-permute-start.71
  523.2 9.1 %collective-permute-done.91 = bf16[192,768]{1,0:T(8,128)(2,1)S(1)} collective-permute-done((bf16[192,768]{1,0:T(8,128)(2,1)S(1)}, bf16[192,768]{1,0:T(8,128)(2,1)S(1)}, u32[]{:S(2)}, u32[]{:S(2)}) %collective-permute-start.91) | collective-permute-done | bytes 294944 | tf_op jit(solution)/shard_map/ppermute | solution.py:898
  533.2 2.6 collective-permute-done.72
  535.8 7.2 %collective-permute-done.71 = bf16[192,768]{1,0:T(8,128)(2,1)S(1)} collective-permute-done((bf16[192,768]{1,0:T(8,128)(2,1)S(1)}, bf16[192,768]{1,0:T(8,128)(2,1)S(1)}, u32[]{:S(2)}, u32[]{:S(2)}) %collective-permute-start.71) | collective-permute-done | bytes 294944 | tf_op jit(solution)/shard_map/ppermute | solution.py:898
  (355 shorter events, 120.6 us)
Async XLA Ops:
  5.0 32.0 %collective-permute-start.4 = (f32[8,768]{1,0:T(8,128)}, f32[8,768]{1,0:T(8,128)}, u32[]{:S(2)}, u32[]{:S(2)}) collective-permute-start(f32[8,768]{1,0:T(8,128)} %concatenate.70), channel_id=1, source_target_pairs={{1,0},{3,1},{0,2},{2,3},{5,4},{7,5},{4,6},{6,7},{9,8},{11,9},{8,10... | collective-permute-start | bytes 73736 | tf_op jit(solution)/shard_map/ppermute | solution.py:890
  5.0 43.7 %collective-permute-start.3 = (f32[8,768]{1,0:T(8,128)}, f32[8,768]{1,0:T(8,128)}, u32[]{:S(2)}, u32[]{:S(2)}) collective-permute-start(f32[8,768]{1,0:T(8,128)} %concatenate.70), channel_id=1, source_target_pairs={{0,0},{2,1},{1,2},{3,3},{4,4},{6,5},{5,6},{7,7},{8,8},{10,9},{9,10... | collective-permute-start | bytes 73736 | tf_op jit(solution)/shard_map/ppermute | solution.py:890
  10.9 12.3 %collective-permute-start.5 = (bf16[192,12]{1,0:T(8,128)(2,1)S(1)}, bf16[192,12]{1,0:T(8,128)(2,1)S(1)}, u32[]{:S(2)}, u32[]{:S(2)}) collective-permute-start(bf16[192,12]{1,0:T(8,128)(2,1)S(1)} %copy.33), channel_id=1, source_target_pairs={{0,0},{2,1},{1,2},{3,3},{4,4},{6,5},{5,6},{7,7},{8,8},{10,9},{9,10... | collective-permute-start | bytes 13832 | tf_op jit(solution)/shard_map/ppermute | solution.py:890
  13.3 12.2 %collective-permute-start.16 = (bf16[192,768]{1,0:T(8,128)(2,1)}, bf16[192,768]{1,0:T(8,128)(2,1)S(1)}, u32[]{:S(2)}, u32[]{:S(2)}) collective-permute-start(bf16[192,768]{1,0:T(8,128)(2,1)} %param.22), channel_id=1, source_target_pairs={{1,0},{3,1},{0,2},{2,3},{5,4},{7,5},{4,6},{6,7},{9,8},{11,9},{8,10... | collective-permute-start | bytes 884744 | tf_op jit(solution)/shard_map/ppermute | solution.py:890
  15.9 13.2 %collective-permute-start.15 = (bf16[192,768]{1,0:T(8,128)(2,1)}, bf16[192,768]{1,0:T(8,128)(2,1)S(1)}, u32[]{:S(2)}, u32[]{:S(2)}) collective-permute-start(bf16[192,768]{1,0:T(8,128)(2,1)} %param.22), channel_id=1, source_target_pairs={{0,0},{2,1},{1,2},{3,3},{4,4},{6,5},{5,6},{7,7},{8,8},{10,9},{9,10... | collective-permute-start | bytes 884744 | tf_op jit(solution)/shard_map/ppermute | solution.py:890
  29.3 16.0 %collective-permute-start.26 = (bf16[192,768]{1,0:T(8,128)(2,1)}, bf16[192,768]{1,0:T(8,128)(2,1)S(1)}, u32[]{:S(2)}, u32[]{:S(2)}) collective-permute-start(bf16[192,768]{1,0:T(8,128)(2,1)} %param.21), channel_id=1, source_target_pairs={{0,0},{2,1},{1,2},{3,3},{4,4},{6,5},{5,6},{7,7},{8,8},{10,9},{9,10... | collective-permute-start | bytes 884744 | tf_op jit(solution)/shard_map/ppermute | solution.py:890
  32.8 16.0 %collective-permute-start.1 = (bf16[16,1536]{1,0:T(8,128)(2,1)S(1)}, bf16[16,1536]{1,0:T(8,128)(2,1)S(1)}, u32[]{:S(2)}, u32[]{:S(2)}) collective-permute-start(bf16[16,1536]{1,0:T(8,128)(2,1)S(1)} %slice.472), channel_id=1, source_target_pairs={{1,3},{5,7},{9,11},{13,15},{17,19},{21,23},{25,27},{29,31}} | collective-permute-start | bytes 147464 | tf_op jit(solution)/shard_map/ppermute | solution.py:1028
  37.0 12.4 %collective-permute-start = (bf16[16,1536]{1,0:T(8,128)(2,1)S(1)}, bf16[16,1536]{1,0:T(8,128)(2,1)S(1)}, u32[]{:S(2)}, u32[]{:S(2)}) collective-permute-start(bf16[16,1536]{1,0:T(8,128)(2,1)S(1)} %slice.472), channel_id=1, source_target_pairs={{1,2},{5,6},{9,10},{13,14},{17,18},{21,22},{25,26},{29,30}} | collective-permute-start | bytes 147464 | tf_op jit(solution)/shard_map/ppermute | solution.py:1028
  46.0 16.4 %collective-permute-start.21 = (bf16[1,192,768]{2,1,0:T(8,128)(2,1)S(1)}, bf16[1,192,768]{2,1,0:T(8,128)(2,1)}, u32[]{:S(2)}, u32[]{:S(2)}) collective-permute-start(bf16[1,192,768]{2,1,0:T(8,128)(2,1)S(1)} %get-tuple-element.154), channel_id=1, source_target_pairs={{0,16},{4,20},{8,24},{12,28},{16,0},{20,4},{24,8},{28,12},{1,17},{... | collective-permute-start | bytes 884744 | tf_op jit(solution)/shard_map/ppermute | solution.py:837
  49.4 15.7 %collective-permute-start.38 = (bf16[192,768]{1,0:T(8,128)(2,1)}, bf16[192,768]{1,0:T(8,128)(2,1)}, u32[]{:S(2)}, u32[]{:S(2)}) collective-permute-start(bf16[192,768]{1,0:T(8,128)(2,1)} %bitcast.90), channel_id=1, source_target_pairs={{1,0},{3,1},{0,2},{2,3},{5,4},{7,5},{4,6},{6,7},{9,8},{11,9},{8,10... | collective-permute-start | bytes 884744 | tf_op jit(solution)/shard_map/ppermute | solution.py:890
  49.4 16.6 %collective-permute-start.37 = (bf16[192,768]{1,0:T(8,128)(2,1)}, bf16[192,768]{1,0:T(8,128)(2,1)}, u32[]{:S(2)}, u32[]{:S(2)}) collective-permute-start(bf16[192,768]{1,0:T(8,128)(2,1)} %bitcast.91), channel_id=1, source_target_pairs={{0,0},{2,1},{1,2},{3,3},{4,4},{6,5},{5,6},{7,7},{8,8},{10,9},{9,10... | collective-permute-start | bytes 884744 | tf_op jit(solution)/shard_map/ppermute | solution.py:890
  66.0 19.0 %collective-permute-start.23 = (bf16[2,192,768]{2,1,0:T(8,128)(2,1)S(1)}, bf16[2,192,768]{2,1,0:T(8,128)(2,1)S(1)}, u32[]{:S(2)}, u32[]{:S(2)}) collective-permute-start(bf16[2,192,768]{2,1,0:T(8,128)(2,1)S(1)} %pad_maximum_fusion.2.rest_4_.rest_12_), channel_id=1, source_target_pairs={{0,4},{4,0},{8,12},{12,8},{16,20},{20,16},{24,28},{28,24},{1,5},{5... | collective-permute-start | bytes 1769480 | tf_op jit(solution)/shard_map/ppermute | solution.py:837
  67.2 32.3 %collective-permute-start.2 = (bf16[384,1536]{1,0:T(8,128)(2,1)S(1)}, bf16[384,1536]{1,0:T(8,128)(2,1)S(1)}, u32[]{:S(2)}, u32[]{:S(2)}) collective-permute-start(bf16[384,1536]{1,0:T(8,128)(2,1)S(1)} %fusion.2), channel_id=1, source_target_pairs={{0,1},{1,0},{2,3},{3,2},{4,5},{5,4},{6,7},{7,6},{8,9},{9,8},{10,11... | collective-permute-start | bytes 3538952 | tf_op jit(solution)/shard_map/ppermute | solution.py:912
  71.9 12.4 %collective-permute-start.39 = (bf16[1,192,768]{2,1,0:T(8,128)(2,1)S(1)}, bf16[1,192,768]{2,1,0:T(8,128)(2,1)S(1)}, u32[]{:S(2)}, u32[]{:S(2)}) collective-permute-start(bf16[1,192,768]{2,1,0:T(8,128)(2,1)S(1)} %get-tuple-element.151), channel_id=1, source_target_pairs={{0,8},{4,12},{8,0},{12,4},{16,24},{20,28},{24,16},{28,20},{1,9},{5... | collective-permute-start | bytes 884744 | tf_op jit(solution)/shard_map/ppermute | solution.py:837
  78.0 18.2 %collective-permute-start.22 = (bf16[2,192,768]{2,1,0:T(8,128)(2,1)S(1)}, bf16[2,192,768]{2,1,0:T(8,128)(2,1)S(1)}, u32[]{:S(2)}, u32[]{:S(2)}) collective-permute-start(bf16[2,192,768]{2,1,0:T(8,128)(2,1)S(1)} %pad_maximum_fusion.2.rest_4_.rest_12_), channel_id=1, source_target_pairs={{0,8},{4,12},{8,0},{12,4},{16,24},{20,28},{24,16},{28,20},{1,9},{5... | collective-permute-start | bytes 1769480 | tf_op jit(solution)/shard_map/ppermute | solution.py:837
  79.5 18.2 %collective-permute-start.19 = (bf16[2,192,768]{2,1,0:T(8,128)(2,1)S(1)}, bf16[2,192,768]{2,1,0:T(8,128)(2,1)S(1)}, u32[]{:S(2)}, u32[]{:S(2)}) collective-permute-start(bf16[2,192,768]{2,1,0:T(8,128)(2,1)S(1)} %pad_maximum_fusion.1.rest_0_.rest_8_), channel_id=1, source_target_pairs={{0,4},{4,0},{8,12},{12,8},{16,20},{20,16},{24,28},{28,24},{1,5},{5... | collective-permute-start | bytes 1769480 | tf_op jit(solution)/shard_map/ppermute | solution.py:837
  84.3 13.8 %collective-permute-start.18 = (bf16[2,192,768]{2,1,0:T(8,128)(2,1)S(1)}, bf16[2,192,768]{2,1,0:T(8,128)(2,1)S(1)}, u32[]{:S(2)}, u32[]{:S(2)}) collective-permute-start(bf16[2,192,768]{2,1,0:T(8,128)(2,1)S(1)} %pad_maximum_fusion.1.rest_0_.rest_8_), channel_id=1, source_target_pairs={{0,16},{4,20},{8,24},{12,28},{16,0},{20,4},{24,8},{28,12},{1,17},{... | collective-permute-start | bytes 1769480 | tf_op jit(solution)/shard_map/ppermute | solution.py:837
  85.0 14.5 %collective-permute-start.34 = (bf16[2,192,768]{2,1,0:T(8,128)(2,1)S(1)}, bf16[2,192,768]{2,1,0:T(8,128)(2,1)S(1)}, u32[]{:S(2)}, u32[]{:S(2)}) collective-permute-start(bf16[2,192,768]{2,1,0:T(8,128)(2,1)S(1)} %pad_maximum_fusion.4.rest_4_), channel_id=1, source_target_pairs={{0,4},{4,0},{8,12},{12,8},{16,20},{20,16},{24,28},{28,24},{1,5},{5... | collective-permute-start | bytes 1769480 | tf_op jit(solution)/shard_map/ppermute | solution.py:837
  96.1 14.7 %collective-permute-start.33 = (bf16[2,192,768]{2,1,0:T(8,128)(2,1)S(1)}, bf16[2,192,768]{2,1,0:T(8,128)(2,1)}, u32[]{:S(2)}, u32[]{:S(2)}) collective-permute-start(bf16[2,192,768]{2,1,0:T(8,128)(2,1)S(1)} %pad_maximum_fusion.4.rest_4_), channel_id=1, source_target_pairs={{0,8},{4,12},{8,0},{12,4},{16,24},{20,28},{24,16},{28,20},{1,9},{5... | collective-permute-start | bytes 1769480 | tf_op jit(solution)/shard_map/ppermute | solution.py:837
  97.6 17.0 %collective-permute-start.30 = (bf16[2,192,768]{2,1,0:T(8,128)(2,1)S(1)}, bf16[2,192,768]{2,1,0:T(8,128)(2,1)S(1)}, u32[]{:S(2)}, u32[]{:S(2)}) collective-permute-start(bf16[2,192,768]{2,1,0:T(8,128)(2,1)S(1)} %pad_maximum_fusion.3.rest_0_), channel_id=1, source_target_pairs={{0,4},{4,0},{8,12},{12,8},{16,20},{20,16},{24,28},{28,24},{1,5},{5... | collective-permute-start | bytes 1769480 | tf_op jit(solution)/shard_map/ppermute | solution.py:837
  98.1 18.1 %collective-permute-start.29 = (bf16[2,192,768]{2,1,0:T(8,128)(2,1)S(1)}, bf16[2,192,768]{2,1,0:T(8,128)(2,1)}, u32[]{:S(2)}, u32[]{:S(2)}) collective-permute-start(bf16[2,192,768]{2,1,0:T(8,128)(2,1)S(1)} %pad_maximum_fusion.3.rest_0_), channel_id=1, source_target_pairs={{0,16},{4,20},{8,24},{12,28},{16,0},{20,4},{24,8},{28,12},{1,17},{... | collective-permute-start | bytes 1769480 | tf_op jit(solution)/shard_map/ppermute | solution.py:837
  99.5 17.4 %collective-permute-start.24 = (bf16[2,192,768]{2,1,0:T(8,128)(2,1)S(1)}, bf16[2,192,768]{2,1,0:T(8,128)(2,1)S(1)}, u32[]{:S(2)}, u32[]{:S(2)}) collective-permute-start(bf16[2,192,768]{2,1,0:T(8,128)(2,1)S(1)} %collective-permute-done.22.rest_5_.rest_13_), channel_id=1, source_target_pairs={{0,4},{4,0},{8,12},{12,8},{16,20},{20,16},{24,28},{28,24},{1,5},{5... | collective-permute-start | bytes 1769480 | tf_op jit(solution)/shard_map/ppermute | solution.py:837
  100.3 16.5 %collective-permute-start.20 = (bf16[2,192,768]{2,1,0:T(8,128)(2,1)S(1)}, bf16[2,192,768]{2,1,0:T(8,128)(2,1)S(1)}, u32[]{:S(2)}, u32[]{:S(2)}) collective-permute-start(bf16[2,192,768]{2,1,0:T(8,128)(2,1)S(1)} %collective-permute-done.18.rest_1_.rest_9_), channel_id=1, source_target_pairs={{0,4},{4,0},{8,12},{12,8},{16,20},{20,16},{24,28},{28,24},{1,5},{5... | collective-permute-start | bytes 1769480 | tf_op jit(solution)/shard_map/ppermute | solution.py:837
  110.8 45.8 %collective-permute-start.36 = (bf16[384,1536]{1,0:T(8,128)(2,1)S(1)}, bf16[384,1536]{1,0:T(8,128)(2,1)S(1)}, u32[]{:S(2)}, u32[]{:S(2)}) collective-permute-start(bf16[384,1536]{1,0:T(8,128)(2,1)S(1)} %copy-done.1), channel_id=1, source_target_pairs={{0,1},{1,0},{2,3},{3,2},{4,5},{5,4},{6,7},{7,6},{8,9},{9,8},{10,11... | collective-permute-start | bytes 3538952 | tf_op jit(solution)/shard_map/ppermute | solution.py:912
  114.7 31.1 %collective-permute-start.40 = (bf16[2,192,768]{2,1,0:T(8,128)(2,1)}, bf16[2,192,768]{2,1,0:T(8,128)(2,1)}, u32[]{:S(2)}, u32[]{:S(2)}) collective-permute-start(bf16[2,192,768]{2,1,0:T(8,128)(2,1)} %pad_maximum_fusion.5.rest_0_), channel_id=1, source_target_pairs={{0,16},{4,20},{8,24},{12,28},{16,0},{20,4},{24,8},{28,12},{1,17},{... | collective-permute-start | bytes 1769480 | tf_op jit(solution)/shard_map/ppermute | solution.py:837
  116.2 29.9 %collective-permute-start.44 = (bf16[2,192,768]{2,1,0:T(8,128)(2,1)}, bf16[2,192,768]{2,1,0:T(8,128)(2,1)}, u32[]{:S(2)}, u32[]{:S(2)}) collective-permute-start(bf16[2,192,768]{2,1,0:T(8,128)(2,1)} %pad_maximum_fusion.6.rest_4_), channel_id=1, source_target_pairs={{0,8},{4,12},{8,0},{12,4},{16,24},{20,28},{24,16},{28,20},{1,9},{5... | collective-permute-start | bytes 1769480 | tf_op jit(solution)/shard_map/ppermute | solution.py:837
  116.8 29.6 %collective-permute-start.35 = (bf16[2,192,768]{2,1,0:T(8,128)(2,1)}, bf16[2,192,768]{2,1,0:T(8,128)(2,1)S(1)}, u32[]{:S(2)}, u32[]{:S(2)}) collective-permute-start(bf16[2,192,768]{2,1,0:T(8,128)(2,1)} %collective-permute-done.33.rest_5_), channel_id=1, source_target_pairs={{0,4},{4,0},{8,12},{12,8},{16,20},{20,16},{24,28},{28,24},{1,5},{5... | collective-permute-start | bytes 1769480 | tf_op jit(solution)/shard_map/ppermute | solution.py:837
  116.9 29.7 %collective-permute-start.31 = (bf16[2,192,768]{2,1,0:T(8,128)(2,1)}, bf16[2,192,768]{2,1,0:T(8,128)(2,1)}, u32[]{:S(2)}, u32[]{:S(2)}) collective-permute-start(bf16[2,192,768]{2,1,0:T(8,128)(2,1)} %collective-permute-done.29.rest_1_), channel_id=1, source_target_pairs={{0,4},{4,0},{8,12},{12,8},{16,20},{20,16},{24,28},{28,24},{1,5},{5... | collective-permute-start | bytes 1769480 | tf_op jit(solution)/shard_map/ppermute | solution.py:837
  145.8 16.6 %collective-permute-start.41 = (bf16[2,192,768]{2,1,0:T(8,128)(2,1)}, bf16[2,192,768]{2,1,0:T(8,128)(2,1)}, u32[]{:S(2)}, u32[]{:S(2)}) collective-permute-start(bf16[2,192,768]{2,1,0:T(8,128)(2,1)} %pad_maximum_fusion.5.rest_0_), channel_id=1, source_target_pairs={{0,4},{4,0},{8,12},{12,8},{16,20},{20,16},{24,28},{28,24},{1,5},{5... | collective-permute-start | bytes 1769480 | tf_op jit(solution)/shard_map/ppermute | solution.py:837
  146.1 16.3 %collective-permute-start.45 = (bf16[2,192,768]{2,1,0:T(8,128)(2,1)}, bf16[2,192,768]{2,1,0:T(8,128)(2,1)}, u32[]{:S(2)}, u32[]{:S(2)}) collective-permute-start(bf16[2,192,768]{2,1,0:T(8,128)(2,1)} %pad_maximum_fusion.6.rest_4_), channel_id=1, source_target_pairs={{0,4},{4,0},{8,12},{12,8},{16,20},{20,16},{24,28},{28,24},{1,5},{5... | collective-permute-start | bytes 1769480 | tf_op jit(solution)/shard_map/ppermute | solution.py:837
  146.4 16.0 %collective-permute-start.42 = (bf16[2,192,768]{2,1,0:T(8,128)(2,1)}, bf16[2,192,768]{2,1,0:T(8,128)(2,1)}, u32[]{:S(2)}, u32[]{:S(2)}) collective-permute-start(bf16[2,192,768]{2,1,0:T(8,128)(2,1)} %collective-permute-done.40.rest_1_), channel_id=1, source_target_pairs={{0,4},{4,0},{8,12},{12,8},{16,20},{20,16},{24,28},{28,24},{1,5},{5... | collective-permute-start | bytes 1769480 | tf_op jit(solution)/shard_map/ppermute | solution.py:837
  146.6 15.8 %collective-permute-start.46 = (bf16[2,192,768]{2,1,0:T(8,128)(2,1)}, bf16[2,192,768]{2,1,0:T(8,128)(2,1)}, u32[]{:S(2)}, u32[]{:S(2)}) collective-permute-start(bf16[2,192,768]{2,1,0:T(8,128)(2,1)} %collective-permute-done.44.rest_5_), channel_id=1, source_target_pairs={{0,4},{4,0},{8,12},{12,8},{16,20},{20,16},{24,28},{28,24},{1,5},{5... | collective-permute-start | bytes 1769480 | tf_op jit(solution)/shard_map/ppermute | solution.py:837
  156.6 21.0 %collective-permute-start.25 = (bf16[128,1536]{1,0:T(8,128)(2,1)}, bf16[128,1536]{1,0:T(8,128)(2,1)S(1)}, u32[]{:S(2)}, u32[]{:S(2)}) collective-permute-start(bf16[128,1536]{1,0:T(8,128)(2,1)} %get-tuple-element.66), channel_id=1, source_target_pairs={{0,2},{1,3},{4,6},{5,7},{8,10},{9,11},{12,14},{13,15},{16,18},{17,... | collective-permute-start | bytes 1179656 | tf_op jit(solution)/shard_map/ppermute | solution.py:1037
  193.0 10.7 %collective-permute-start.47 = (f32[768,128]{1,0:T(8,128)}, f32[768,128]{1,0:T(8,128)S(1)}, u32[]{:S(2)}, u32[]{:S(2)}) collective-permute-start(f32[768,128]{1,0:T(8,128)} %get-tuple-element.71.stat_a), channel_id=1, source_target_pairs={{0,1},{1,0},{2,3},{3,2},{4,5},{5,4},{6,7},{7,6},{8,9},{9,8},{10,11... | collective-permute-start | bytes 1179656 | tf_op jit(solution)/shard_map/ppermute | solution.py:924
  218.2 12.6 %collective-permute-start.49 = (bf16[128,1536]{1,0:T(8,128)(2,1)}, bf16[128,1536]{1,0:T(8,128)(2,1)S(1)}, u32[]{:S(2)}, u32[]{:S(2)}) collective-permute-start(bf16[128,1536]{1,0:T(8,128)(2,1)} %get-tuple-element.77), channel_id=1, source_target_pairs={{2,0},{3,1},{6,4},{7,5},{10,8},{11,9},{14,12},{15,13},{18,16},{19,... | collective-permute-start | bytes 1179656 | tf_op jit(solution)/shard_map/ppermute | solution.py:1045
  283.2 11.9 %collective-permute-start.82 = (f32[8,1536]{1,0:T(8,128)S(1)}, f32[8,1536]{1,0:T(8,128)S(1)}, u32[]{:S(2)}, u32[]{:S(2)}) collective-permute-start(f32[8,1536]{1,0:T(8,128)S(1)} %fusion.18), channel_id=1, source_target_pairs={{0,8},{4,12},{8,0},{12,4},{16,24},{20,28},{24,16},{28,20},{1,9},{5... | collective-permute-start | bytes 147464 | tf_op jit(solution)/shard_map/ppermute | solution.py:837
  286.2 158.6 %collective-permute-start.48 = (bf16[384,1536]{1,0:T(8,128)(2,1)}, bf16[384,1536]{1,0:T(8,128)(2,1)}, u32[]{:S(2)}, u32[]{:S(2)}) collective-permute-start(bf16[384,1536]{1,0:T(8,128)(2,1)} %constant_dynamic-slice_fusion.1), channel_id=1, source_target_pairs={{0,1},{1,0},{2,3},{3,2},{4,5},{5,4},{6,7},{7,6},{8,9},{9,8},{10,11... | collective-permute-start | bytes 3538952 | tf_op jit(solution)/shard_map/ppermute | solution.py:935
  295.1 10.9 %collective-permute-start.83 = (f32[8,1536]{1,0:T(8,128)S(1)}, f32[8,1536]{1,0:T(8,128)S(1)}, u32[]{:S(2)}, u32[]{:S(2)}) collective-permute-start(f32[8,1536]{1,0:T(8,128)S(1)} %add.421), channel_id=1, source_target_pairs={{0,16},{4,20},{8,24},{12,28},{16,0},{20,4},{24,8},{28,12},{1,17},{... | collective-permute-start | bytes 147464 | tf_op jit(solution)/shard_map/ppermute | solution.py:837
  304.7 144.7 %collective-permute-start.59 = (bf16[4,192,1536]{2,1,0:T(8,128)(2,1)}, bf16[4,192,1536]{2,1,0:T(8,128)(2,1)}, u32[]{:S(2)}, u32[]{:S(2)}) collective-permute-start(bf16[4,192,1536]{2,1,0:T(8,128)(2,1)} %get-tuple-element.88), channel_id=1, source_target_pairs={{0,4},{4,0},{8,12},{12,8},{16,20},{20,16},{24,28},{28,24},{1,5},{5... | collective-permute-start | bytes 7077896 | tf_op jit(solution)/shard_map/ppermute | solution.py:837
  304.8 25.8 %collective-permute-start.50 = (bf16[768,256]{1,0:T(8,128)(2,1)S(1)}, bf16[768,256]{1,0:T(8,128)(2,1)S(1)}, u32[]{:S(2)}, u32[]{:S(2)}) collective-permute-start(bf16[768,256]{1,0:T(8,128)(2,1)S(1)} %convert_element_type.535.own), channel_id=1, source_target_pairs={{0,1},{1,0},{2,3},{3,2},{4,5},{5,4},{6,7},{7,6},{8,9},{9,8},{10,11... | collective-permute-start | bytes 1179656 | tf_op jit(solution)/shard_map/ppermute | solution.py:924
  306.1 24.5 %collective-permute-start.85 = (f32[8,768]{1,0:T(8,128)S(1)}, f32[8,768]{1,0:T(8,128)S(1)}, u32[]{:S(2)}, u32[]{:S(2)}) collective-permute-start(f32[8,768]{1,0:T(8,128)S(1)} %get-tuple-element.158), channel_id=1, source_target_pairs={{0,1},{1,3},{2,0},{3,2},{4,5},{5,7},{6,4},{7,6},{8,9},{9,11},{10,8... | collective-permute-start | bytes 73736 | tf_op jit(solution)/shard_map/ppermute | solution.py:899
  306.1 24.4 %collective-permute-start.84 = (f32[8,768]{1,0:T(8,128)S(1)}, f32[8,768]{1,0:T(8,128)S(1)}, u32[]{:S(2)}, u32[]{:S(2)}) collective-permute-start(f32[8,768]{1,0:T(8,128)S(1)} %get-tuple-element.159), channel_id=1, source_target_pairs={{0,0},{1,2},{2,1},{3,3},{4,4},{5,6},{6,5},{7,7},{8,8},{9,10},{10,9... | collective-permute-start | bytes 73736 | tf_op jit(solution)/shard_map/ppermute | solution.py:898
  365.0 13.2 %collective-permute-start.53 = (bf16[16,1536]{1,0:T(8,128)(2,1)S(1)}, bf16[16,1536]{1,0:T(8,128)(2,1)S(1)}, u32[]{:S(2)}, u32[]{:S(2)}) collective-permute-start(bf16[16,1536]{1,0:T(8,128)(2,1)S(1)} %slice.371), channel_id=1, source_target_pairs={{3,1},{7,5},{11,9},{15,13},{19,17},{23,21},{27,25},{31,29}} | collective-permute-start | bytes 147464 | tf_op jit(solution)/shard_map/ppermute | solution.py:1064
  366.3 13.5 %collective-permute-start.52 = (bf16[16,1536]{1,0:T(8,128)(2,1)S(1)}, bf16[16,1536]{1,0:T(8,128)(2,1)S(1)}, u32[]{:S(2)}, u32[]{:S(2)}) collective-permute-start(bf16[16,1536]{1,0:T(8,128)(2,1)S(1)} %slice.371), channel_id=1, source_target_pairs={{2,1},{6,5},{10,9},{14,13},{18,17},{22,21},{26,25},{30,29}} | collective-permute-start | bytes 147464 | tf_op jit(solution)/shard_map/ppermute | solution.py:1064
  378.1 32.0 %collective-permute-start.73 = (bf16[4,192,384]{2,1,0:T(8,128)(2,1)}, bf16[4,192,384]{2,1,0:T(8,128)(2,1)S(1)}, u32[]{:S(2)}, u32[]{:S(2)}) collective-permute-start(bf16[4,192,384]{2,1,0:T(8,128)(2,1)} %get-tuple-element.92), channel_id=1, source_target_pairs={{0,4},{4,0},{8,12},{12,8},{16,20},{20,16},{24,28},{28,24},{1,5},{5... | collective-permute-start | bytes 1769480 | tf_op jit(solution)/shard_map/ppermute | solution.py:837
  378.2 64.7 %collective-permute-start.51 = (bf16[384,1536]{1,0:T(8,128)(2,1)}, bf16[384,1536]{1,0:T(8,128)(2,1)}, u32[]{:S(2)}, u32[]{:S(2)}) collective-permute-start(bf16[384,1536]{1,0:T(8,128)(2,1)} %constant_dynamic-slice_fusion), channel_id=1, source_target_pairs={{0,1},{1,0},{2,3},{3,2},{4,5},{5,4},{6,7},{7,6},{8,9},{9,8},{10,11... | collective-permute-start | bytes 3538952 | tf_op jit(solution)/shard_map/ppermute | solution.py:935
  379.8 29.7 %collective-permute-start.58 = (f32[22,128]{1,0:T(8,128)S(1)}, f32[22,128]{1,0:T(8,128)S(1)}, u32[]{:S(2)}, u32[]{:S(2)}) collective-permute-start(f32[22,128]{1,0:T(8,128)S(1)} %add.366), channel_id=1, source_target_pairs={{0,2},{1,3},{2,0},{3,1},{4,6},{5,7},{6,4},{7,5},{8,10},{9,11},{10,... | collective-permute-start | bytes 33800 | tf_op jit(solution)/shard_map/ppermute | solution.py:950
  428.5 24.5 %collective-permute-start.86 = (bf16[4,192,1536]{2,1,0:T(8,128)(2,1)}, bf16[4,192,1536]{2,1,0:T(8,128)(2,1)}, u32[]{:S(2)}, u32[]{:S(2)}) collective-permute-start(bf16[4,192,1536]{2,1,0:T(8,128)(2,1)} %get-tuple-element.97), channel_id=1, source_target_pairs={{0,4},{4,0},{8,12},{12,8},{16,20},{20,16},{24,28},{28,24},{1,5},{5... | collective-permute-start | bytes 7077896 | tf_op jit(solution)/shard_map/ppermute | solution.py:837
  441.2 16.2 %collective-permute-start.66 = (bf16[4,192,1536]{2,1,0:T(8,128)(2,1)}, bf16[4,192,1536]{2,1,0:T(8,128)(2,1)S(1)}, u32[]{:S(2)}, u32[]{:S(2)}) collective-permute-start(bf16[4,192,1536]{2,1,0:T(8,128)(2,1)} %get-tuple-element.90), channel_id=1, source_target_pairs={{0,4},{4,0},{8,12},{12,8},{16,20},{20,16},{24,28},{28,24},{1,5},{5... | collective-permute-start | bytes 7077896 | tf_op jit(solution)/shard_map/ppermute | solution.py:837
  451.2 16.2 %collective-permute-start.60 = (bf16[2,192,768]{2,1,0:T(8,128)(2,1)S(1)}, bf16[2,192,768]{2,1,0:T(8,128)(2,1)S(1)}, u32[]{:S(2)}, u32[]{:S(2)}) collective-permute-start(bf16[2,192,768]{2,1,0:T(8,128)(2,1)S(1)} %pad_maximum_fusion.7), channel_id=1, source_target_pairs={{0,8},{4,12},{8,0},{12,4},{16,24},{20,28},{24,16},{28,20},{1,9},{5... | collective-permute-start | bytes 1769480 | tf_op jit(solution)/shard_map/ppermute | solution.py:837
  451.8 16.2 %collective-permute-start.62 = (bf16[2,192,768]{2,1,0:T(8,128)(2,1)S(1)}, bf16[2,192,768]{2,1,0:T(8,128)(2,1)S(1)}, u32[]{:S(2)}, u32[]{:S(2)}) collective-permute-start(bf16[2,192,768]{2,1,0:T(8,128)(2,1)S(1)} %pad_maximum_fusion.8), channel_id=1, source_target_pairs={{0,16},{4,20},{8,24},{12,28},{16,0},{20,4},{24,8},{28,12},{1,17},{... | collective-permute-start | bytes 1769480 | tf_op jit(solution)/shard_map/ppermute | solution.py:837
  454.8 25.2 %collective-permute-start.87 = (bf16[2,192,768]{2,1,0:T(8,128)(2,1)S(1)}, bf16[2,192,768]{2,1,0:T(8,128)(2,1)S(1)}, u32[]{:S(2)}, u32[]{:S(2)}) collective-permute-start(bf16[2,192,768]{2,1,0:T(8,128)(2,1)S(1)} %pad_maximum_fusion.11), channel_id=1, source_target_pairs={{0,8},{4,12},{8,0},{12,4},{16,24},{20,28},{24,16},{28,20},{1,9},{5... | collective-permute-start | bytes 1769480 | tf_op jit(solution)/shard_map/ppermute | solution.py:837
  456.4 24.7 %collective-permute-start.89 = (bf16[2,192,768]{2,1,0:T(8,128)(2,1)S(1)}, bf16[2,192,768]{2,1,0:T(8,128)(2,1)S(1)}, u32[]{:S(2)}, u32[]{:S(2)}) collective-permute-start(bf16[2,192,768]{2,1,0:T(8,128)(2,1)S(1)} %pad_maximum_fusion.12), channel_id=1, source_target_pairs={{0,16},{4,20},{8,24},{12,28},{16,0},{20,4},{24,8},{28,12},{1,17},{... | collective-permute-start | bytes 1769480 | tf_op jit(solution)/shard_map/ppermute | solution.py:837
  457.8 45.3 %collective-permute-start.67 = (bf16[2,192,768]{2,1,0:T(8,128)(2,1)S(1)}, bf16[2,192,768]{2,1,0:T(8,128)(2,1)S(1)}, u32[]{:S(2)}, u32[]{:S(2)}) collective-permute-start(bf16[2,192,768]{2,1,0:T(8,128)(2,1)S(1)} %pad_maximum_fusion.9), channel_id=1, source_target_pairs={{0,8},{4,12},{8,0},{12,4},{16,24},{20,28},{24,16},{28,20},{1,9},{5... | collective-permute-start | bytes 1769480 | tf_op jit(solution)/shard_map/ppermute | solution.py:837
  469.3 29.6 %collective-permute-start.63 = (bf16[1,192,768]{2,1,0:T(8,128)(2,1)S(1)}, bf16[1,192,768]{2,1,0:T(8,128)(2,1)S(1)}, u32[]{:S(2)}, u32[]{:S(2)}) collective-permute-start(bf16[1,192,768]{2,1,0:T(8,128)(2,1)S(1)} %get-tuple-element.138), channel_id=1, source_target_pairs={{0,8},{4,12},{8,0},{12,4},{16,24},{20,28},{24,16},{28,20},{1,9},{5... | collective-permute-start | bytes 884744 | tf_op jit(solution)/shard_map/ppermute | solution.py:837
  470.9 29.1 %collective-permute-start.61 = (bf16[1,192,768]{2,1,0:T(8,128)(2,1)S(1)}, bf16[1,192,768]{2,1,0:T(8,128)(2,1)S(1)}, u32[]{:S(2)}, u32[]{:S(2)}) collective-permute-start(bf16[1,192,768]{2,1,0:T(8,128)(2,1)S(1)} %get-tuple-element.139), channel_id=1, source_target_pairs={{0,16},{4,20},{8,24},{12,28},{16,0},{20,4},{24,8},{28,12},{1,17},{... | collective-permute-start | bytes 884744 | tf_op jit(solution)/shard_map/ppermute | solution.py:837
  480.0 27.3 %collective-permute-start.69 = (bf16[2,192,768]{2,1,0:T(8,128)(2,1)S(1)}, bf16[2,192,768]{2,1,0:T(8,128)(2,1)S(1)}, u32[]{:S(2)}, u32[]{:S(2)}) collective-permute-start(bf16[2,192,768]{2,1,0:T(8,128)(2,1)S(1)} %pad_maximum_fusion.10), channel_id=1, source_target_pairs={{0,16},{4,20},{8,24},{12,28},{16,0},{20,4},{24,8},{28,12},{1,17},{... | collective-permute-start | bytes 1769480 | tf_op jit(solution)/shard_map/ppermute | solution.py:837
  482.4 25.8 %collective-permute-start.90 = (bf16[1,192,768]{2,1,0:T(8,128)(2,1)S(1)}, bf16[1,192,768]{2,1,0:T(8,128)(2,1)S(1)}, u32[]{:S(2)}, u32[]{:S(2)}) collective-permute-start(bf16[1,192,768]{2,1,0:T(8,128)(2,1)S(1)} %get-tuple-element.126), channel_id=1, source_target_pairs={{0,8},{4,12},{8,0},{12,4},{16,24},{20,28},{24,16},{28,20},{1,9},{5... | collective-permute-start | bytes 884744 | tf_op jit(solution)/shard_map/ppermute | solution.py:837
  501.5 16.2 %collective-permute-start.65 = (bf16[192,768]{1,0:T(8,128)(2,1)S(1)}, bf16[192,768]{1,0:T(8,128)(2,1)S(1)}, u32[]{:S(2)}, u32[]{:S(2)}) collective-permute-start(bf16[192,768]{1,0:T(8,128)(2,1)S(1)} %select_bitcast_fusion.4), channel_id=1, source_target_pairs={{0,1},{1,3},{2,0},{3,2},{4,5},{5,7},{6,4},{7,6},{8,9},{9,11},{10,8... | collective-permute-start | bytes 884744 | tf_op jit(solution)/shard_map/ppermute | solution.py:899
  503.1 18.3 %collective-permute-start.64 = (bf16[192,768]{1,0:T(8,128)(2,1)S(1)}, bf16[192,768]{1,0:T(8,128)(2,1)S(1)}, u32[]{:S(2)}, u32[]{:S(2)}) collective-permute-start(bf16[192,768]{1,0:T(8,128)(2,1)S(1)} %get-tuple-element.123), channel_id=1, source_target_pairs={{0,0},{1,2},{2,1},{3,3},{4,4},{5,6},{6,5},{7,7},{8,8},{9,10},{10,9... | collective-permute-start | bytes 884744 | tf_op jit(solution)/shard_map/ppermute | solution.py:898
  510.6 12.6 %collective-permute-start.92 = (bf16[192,768]{1,0:T(8,128)(2,1)S(1)}, bf16[192,768]{1,0:T(8,128)(2,1)S(1)}, u32[]{:S(2)}, u32[]{:S(2)}) collective-permute-start(bf16[192,768]{1,0:T(8,128)(2,1)S(1)} %select_bitcast_fusion), channel_id=1, source_target_pairs={{0,1},{1,3},{2,0},{3,2},{4,5},{5,7},{6,4},{7,6},{8,9},{9,11},{10,8... | collective-permute-start | bytes 884744 | tf_op jit(solution)/shard_map/ppermute | solution.py:899
  515.1 17.2 %collective-permute-start.91 = (bf16[192,768]{1,0:T(8,128)(2,1)S(1)}, bf16[192,768]{1,0:T(8,128)(2,1)S(1)}, u32[]{:S(2)}, u32[]{:S(2)}) collective-permute-start(bf16[192,768]{1,0:T(8,128)(2,1)S(1)} %get-tuple-element.117), channel_id=1, source_target_pairs={{0,0},{1,2},{2,1},{3,3},{4,4},{5,6},{6,5},{7,7},{8,8},{9,10},{10,9... | collective-permute-start | bytes 884744 | tf_op jit(solution)/shard_map/ppermute | solution.py:898
  517.7 18.1 %collective-permute-start.72 = (bf16[192,768]{1,0:T(8,128)(2,1)S(1)}, bf16[192,768]{1,0:T(8,128)(2,1)S(1)}, u32[]{:S(2)}, u32[]{:S(2)}) collective-permute-start(bf16[192,768]{1,0:T(8,128)(2,1)S(1)} %select_bitcast_fusion.2), channel_id=1, source_target_pairs={{0,1},{1,3},{2,0},{3,2},{4,5},{5,7},{6,4},{7,6},{8,9},{9,11},{10,8... | collective-permute-start | bytes 884744 | tf_op jit(solution)/shard_map/ppermute | solution.py:899
  517.8 25.2 %collective-permute-start.71 = (bf16[192,768]{1,0:T(8,128)(2,1)S(1)}, bf16[192,768]{1,0:T(8,128)(2,1)S(1)}, u32[]{:S(2)}, u32[]{:S(2)}) collective-permute-start(bf16[192,768]{1,0:T(8,128)(2,1)S(1)} %get-tuple-element.120), channel_id=1, source_target_pairs={{0,0},{1,2},{2,1},{3,3},{4,4},{5,6},{6,5},{7,7},{8,8},{9,10},{10,9... | collective-permute-start | bytes 884744 | tf_op jit(solution)/shard_map/ppermute | solution.py:898
  (81 other events, 794.2 us)
